TPU v7x, 32 devices: a whole 2x2x4 slice. The times are simulated.
32 devices in a mesh: row: 4 (over x, core), seq: 8 (over z, y).
Axes of the slice: x: 2, y: 2, z: 4, core: 2. Of those that a mesh axis runs over, the one named last changes fastest.
Arguments:
- tokens: bfloat16 [8, 512, 1024], P('row', 'seq'), may hold values from -6 to 6
- memory: bfloat16 [8, 1024, 1024], P('row', 'seq'), may hold values from -6 to 6
- source_len: int32 [8], P('row'), may hold values from 1 to 1024, as said below
- bucket_order: int32 [16], replicated, may hold values from 0 to 15, each once
- prefix_self: float32 [2, 30, 1024], replicated, may hold values from -6 to 6
- prefix_cross: float32 [2, 30, 1024], replicated, may hold values from -6 to 6
- self_query: float32 [1024, 1024], P('row'), may hold values from -0.375 to 0.375
- self_kv: float32 [2, 1024, 1024], P(None, 'row'), may hold values from -0.1875 to 0.1875
- self_out: float32 [1024, 1024], P('row'), may hold values from -0.75 to 0.75
- cross_query: float32 [1024, 1024], P('row'), may hold values from -0.375 to 0.375
- cross_kv: float32 [2, 1024, 1024], P(None, 'row'), may hold values from -0.1875 to 0.1875
- cross_out: float32 [1024, 1024], P('row'), may hold values from -0.75 to 0.75
- fc_in: float32 [1024, 4096], P('row'), may hold values from -0.1875 to 0.1875
- fc_out: float32 [4096, 1024], P('row'), may hold values from -0.09375 to 0.09375
- ln_gain: float32 [3, 1024], replicated, may hold values from 0.5 to 1.5
- ln_bias: float32 [3, 1024], replicated, may hold values from -1.25 to 1.25
- ad_down: float32 [1024, 512], replicated, may hold values from -0.1875 to 0.1875
- ad_down_bias: float32 [512], replicated, may hold values from -3 to 3
- ad_up: float32 [512, 1024], replicated, may hold values from -0.125 to 0.125
- ad_up_bias: float32 [1024], replicated, may hold values from -1.5 to 1.5
- cotangent: bfloat16 [8, 512, 1024], P('row', 'seq'), may hold values from -6 to 6
Outputs:
- mixed: bfloat16 [8, 512, 1024], P('row', 'seq')
- d_tokens: bfloat16 [8, 512, 1024], P('row', 'seq')
- d_memory: bfloat16 [8, 1024, 1024], P('row', 'seq')
- grad_prefix_self: float32 [2, 30, 1024], replicated
- grad_prefix_cross: float32 [2, 30, 1024], replicated
- grad_ad_down: float32 [1024, 512], replicated
- grad_ad_down_bias: float32 [512], replicated
- grad_ad_up: float32 [512, 1024], replicated
- grad_ad_up_bias: float32 [1024], replicated
Inputs may be any that keep to these rules, and one draw needn't show every extreme that they name: `source_len`: in every group of 2 sequences on one index of row one sequence has all 1024 slots live, the others fewer than 409. A permutation; index s of seq stores buckets bucket_order[2 s] and bucket_order[2 s + 1] of every sequence, each of 32 tokens.
All inputs are finite; a program needn't handle non-finite values.
Results may differ from a plain program's by a relative error of at most 0.025.
The roundings to bfloat16 on the way count: a program that leaves them out, or rounds other values in their place, can miss the bound.
Values may be sent and summed in bfloat16 or wider, within the bound.
No kernel may reach another device: no remote copies, remote signals or barrier semaphores. Data moves between devices by JAX's collectives and lax.ppermute only.
A program may use at most 384 MiB of HBM per device.

v0:
```python
import jax
import jax.numpy as jnp
from jax import lax
from jax.sharding import PartitionSpec as P

H = 16
HD = 64


EPSILON = 1e-05
MASKED = -1e30


def normalize(value, gain, shift):
    centre = value - jnp.mean(value, axis=-1, keepdims=True)
    inv_dev = lax.rsqrt(jnp.mean(centre * centre, axis=-1, keepdims=True) + EPSILON)
    unit_val = centre * inv_dev
    return (unit_val * gain + shift, unit_val, inv_dev)


def normalize_back(grad, unit_val, inv_dev, gain):
    scaled = grad * gain
    return inv_dev * (
        scaled
        - jnp.mean(scaled, axis=-1, keepdims=True)
        - unit_val * jnp.mean(scaled * unit_val, axis=-1, keepdims=True)
    )


def gelu_exact(value):
    return jax.nn.gelu(value, approximate=False)


def gelu_back(value, grad):
    return jax.vjp(gelu_exact, value)[1](grad)[0]


def head_split(matrix):
    return matrix.reshape(matrix.shape[0], H, HD)


def masked_scores(queries, keys, mask):
    scores = jnp.einsum(
        "qhd,khd->hqk", head_split(queries), head_split(keys), preferred_element_type=jnp.float32
    )
    return jnp.where(mask[None], scores, MASKED)


def attend(queries, keys, values, mask):
    scores = masked_scores(queries, keys, mask)
    top_score = jnp.max(scores, axis=-1, keepdims=True)
    log_total = top_score + jnp.log(jnp.sum(jnp.exp(scores - top_score), axis=-1, keepdims=True))
    probs = jnp.exp(scores - log_total).astype(jnp.bfloat16)
    result = jnp.einsum(
        "hqk,khd->qhd", probs, head_split(values), preferred_element_type=jnp.float32
    )
    return (result.reshape(queries.shape[0], -1), log_total)


def attend_back(queries, keys, values, mask, log_total, grad_out):
    probs = jnp.exp(masked_scores(queries, keys, mask) - log_total)
    grad_heads = head_split(grad_out)
    grad_probs = jnp.einsum(
        "qhd,khd->hqk", grad_heads, head_split(values), preferred_element_type=jnp.float32
    )
    row_delta = jnp.sum(probs * grad_probs, axis=-1, keepdims=True)
    grad_scores = (probs * (grad_probs - row_delta)).astype(jnp.bfloat16)
    grad_query = jnp.einsum(
        "hqk,khd->qhd", grad_scores, head_split(keys), preferred_element_type=jnp.float32
    )
    grad_keys = jnp.einsum(
        "hqk,qhd->khd", grad_scores, head_split(queries), preferred_element_type=jnp.float32
    )
    grad_values = jnp.einsum(
        "hqk,qhd->khd", probs.astype(jnp.bfloat16), grad_heads, preferred_element_type=jnp.float32
    )
    return (
        grad_query.reshape(queries.shape[0], -1),
        grad_keys.reshape(keys.shape[0], -1),
        grad_values.reshape(values.shape[0], -1),
    )


def project(left, right):
    return jnp.dot(left, right, preferred_element_type=jnp.float32)


def local(
    tokens,
    memory,
    source_len,
    bucket_order,
    prefix_self,
    prefix_cross,
    self_query,
    self_kv,
    self_out,
    cross_query,
    cross_kv,
    cross_out,
    fc_in,
    fc_out,
    ln_gain,
    ln_bias,
    ad_down,
    ad_down_bias,
    ad_up,
    ad_up_bias,
    cotangent,
):
    low_type = jnp.bfloat16
    row_count, tok_count, width = tokens.shape
    slot_count = memory.shape[1]
    prefix_count = prefix_self.shape[1]
    half_len = tok_count // 2
    scale = HD ** (-0.5)
    weight_set = (
        lax.all_gather(self_query.astype(low_type), "row", axis=0, tiled=True),
        lax.all_gather(self_kv.astype(low_type), "row", axis=1, tiled=True),
        lax.all_gather(self_out.astype(low_type), "row", axis=0, tiled=True),
        lax.all_gather(cross_query.astype(low_type), "row", axis=0, tiled=True),
        lax.all_gather(cross_kv.astype(low_type), "row", axis=1, tiled=True),
        lax.all_gather(cross_out.astype(low_type), "row", axis=0, tiled=True),
        lax.all_gather(fc_in.astype(low_type), "row", axis=0, tiled=True),
        lax.all_gather(fc_out.astype(low_type), "row", axis=0, tiled=True),
    )
    q_weight, kv_weight, o_weight, cq_weight, ckv_weight, co_weight, in_weight, out_weight = (
        weight_set
    )
    place = lax.axis_index("seq")
    offsets = jnp.arange(half_len, dtype=jnp.int32)
    all_pos = (bucket_order[:, None] * half_len + offsets[None, :]).reshape(-1)
    own_pos = lax.dynamic_slice_in_dim(all_pos, place * tok_count, tok_count)
    self_mask = jnp.concatenate(
        [jnp.ones((tok_count, prefix_count), jnp.bool_), all_pos[None, :] <= own_pos[:, None]],
        axis=1,
    )
    flat_tokens = tokens.reshape(-1, width)
    queries = (project(flat_tokens, q_weight) * scale).astype(low_type)
    own_keys = (
        project(flat_tokens, kv_weight[0]).astype(low_type).reshape(row_count, tok_count, width)
    )
    own_values = (
        project(flat_tokens, kv_weight[1]).astype(low_type).reshape(row_count, tok_count, width)
    )
    flat_memory = memory.reshape(-1, width)
    mem_keys = (
        project(flat_memory, ckv_weight[0]).astype(low_type).reshape(row_count, slot_count, width)
    )
    mem_values = (
        project(flat_memory, ckv_weight[1]).astype(low_type).reshape(row_count, slot_count, width)
    )
    all_keys, all_values, all_mkeys, all_mvalues = (
        lax.all_gather(own_keys, "seq", axis=1, tiled=True),
        lax.all_gather(own_values, "seq", axis=1, tiled=True),
        lax.all_gather(mem_keys, "seq", axis=1, tiled=True),
        lax.all_gather(mem_values, "seq", axis=1, tiled=True),
    )
    src_total = all_mkeys.shape[1]
    pre_self = prefix_self.astype(low_type)
    pre_cross = prefix_cross.astype(low_type)
    self_key_sets = [
        jnp.concatenate([pre_self[0], all_keys[row_index]], 0) for row_index in range(row_count)
    ]
    self_value_sets = [
        jnp.concatenate([pre_self[1], all_values[row_index]], 0) for row_index in range(row_count)
    ]
    cross_key_sets = [
        jnp.concatenate([pre_cross[0], all_mkeys[row_index]], 0) for row_index in range(row_count)
    ]
    cross_value_sets = [
        jnp.concatenate([pre_cross[1], all_mvalues[row_index]], 0) for row_index in range(row_count)
    ]
    slot_number = jnp.arange(src_total, dtype=jnp.int32)
    cross_masks = [
        jnp.concatenate(
            [jnp.ones((prefix_count,), jnp.bool_), slot_number < source_len[row_index]]
        )[None, :]
        for row_index in range(row_count)
    ]

    def rows_of(matrix, row_index):
        return matrix[row_index * tok_count : (row_index + 1) * tok_count]

    self_parts = [
        attend(
            rows_of(queries, row_index),
            self_key_sets[row_index],
            self_value_sets[row_index],
            self_mask,
        )
        for row_index in range(row_count)
    ]
    attended = jnp.concatenate([part[0] for part in self_parts], 0).astype(low_type)
    resid_one = flat_tokens.astype(jnp.float32) + project(attended, o_weight)
    hidden_one, unit_one, inv_one = normalize(resid_one, ln_gain[0], ln_bias[0])
    cross_queries = (project(hidden_one.astype(low_type), cq_weight) * scale).astype(low_type)
    cross_parts = [
        attend(
            rows_of(cross_queries, row_index),
            cross_key_sets[row_index],
            cross_value_sets[row_index],
            cross_masks[row_index],
        )
        for row_index in range(row_count)
    ]
    cross_att = jnp.concatenate([part[0] for part in cross_parts], 0).astype(low_type)
    resid_two = hidden_one + project(cross_att, co_weight)
    hidden_two, unit_two, inv_two = normalize(resid_two, ln_gain[1], ln_bias[1])
    hidden_low = hidden_two.astype(low_type)
    up_proj = project(hidden_low, in_weight)
    activated = gelu_exact(up_proj).astype(low_type)
    ffn_out = project(activated, out_weight)
    down_weight = ad_down.astype(low_type)
    up_weight = ad_up.astype(low_type)
    down_proj = project(hidden_low, down_weight) + ad_down_bias
    down_act = gelu_exact(down_proj).astype(low_type)
    adapted = project(down_act, up_weight) + ad_up_bias
    resid_three = hidden_two + ffn_out + 4.0 * adapted
    output, unit_three, inv_three = normalize(resid_three, ln_gain[2], ln_bias[2])
    mixed = output.astype(low_type).reshape(row_count, tok_count, width)
    weight_set = (
        lax.all_gather(self_query.astype(low_type), "row", axis=0, tiled=True),
        lax.all_gather(self_kv.astype(low_type), "row", axis=1, tiled=True),
        lax.all_gather(self_out.astype(low_type), "row", axis=0, tiled=True),
        lax.all_gather(cross_query.astype(low_type), "row", axis=0, tiled=True),
        lax.all_gather(cross_kv.astype(low_type), "row", axis=1, tiled=True),
        lax.all_gather(cross_out.astype(low_type), "row", axis=0, tiled=True),
        lax.all_gather(fc_in.astype(low_type), "row", axis=0, tiled=True),
        lax.all_gather(fc_out.astype(low_type), "row", axis=0, tiled=True),
    )
    q_weight, kv_weight, o_weight, cq_weight, ckv_weight, co_weight, in_weight, out_weight = (
        weight_set
    )
    grad_out = cotangent.astype(jnp.float32).reshape(-1, width)
    grad_three = normalize_back(grad_out, unit_three, inv_three, ln_gain[2])
    grad_ffn = grad_three.astype(low_type)
    grad_adapt = (4.0 * grad_three).astype(low_type)
    grad_up_w = jnp.einsum("na,nd->ad", down_act, grad_adapt, preferred_element_type=jnp.float32)
    grad_up_b = jnp.sum(grad_adapt.astype(jnp.float32), axis=0)
    grad_down = gelu_back(down_proj, project(grad_adapt, up_weight.T)).astype(low_type)
    grad_down_w = jnp.einsum("nd,na->da", hidden_low, grad_down, preferred_element_type=jnp.float32)
    grad_down_b = jnp.sum(grad_down.astype(jnp.float32), axis=0)
    grad_inner = gelu_back(up_proj, project(grad_ffn, out_weight.T)).astype(low_type)
    grad_hidden_two = (
        grad_three + project(grad_inner, in_weight.T) + project(grad_down, down_weight.T)
    )
    grad_two = normalize_back(grad_hidden_two, unit_two, inv_two, ln_gain[1])
    grad_cross_att = project(grad_two.astype(low_type), co_weight.T).astype(low_type)
    cross_grads = [
        attend_back(
            rows_of(cross_queries, row_index),
            cross_key_sets[row_index],
            cross_value_sets[row_index],
            cross_masks[row_index],
            cross_parts[row_index][1],
            rows_of(grad_cross_att, row_index),
        )
        for row_index in range(row_count)
    ]
    grad_cq = jnp.concatenate([part[0] for part in cross_grads], 0).astype(low_type)
    grad_hidden_one = grad_two + project(grad_cq, cq_weight.T) * scale
    grad_one = normalize_back(grad_hidden_one, unit_one, inv_one, ln_gain[0])
    grad_attended = project(grad_one.astype(low_type), o_weight.T).astype(low_type)
    self_grads = [
        attend_back(
            rows_of(queries, row_index),
            self_key_sets[row_index],
            self_value_sets[row_index],
            self_mask,
            self_parts[row_index][1],
            rows_of(grad_attended, row_index),
        )
        for row_index in range(row_count)
    ]
    pre_self_grad = jnp.stack(
        [
            sum((part[1][:prefix_count] for part in self_grads)),
            sum((part[2][:prefix_count] for part in self_grads)),
        ]
    )
    pre_cross_grad = jnp.stack(
        [
            sum((part[1][:prefix_count] for part in cross_grads)),
            sum((part[2][:prefix_count] for part in cross_grads)),
        ]
    )
    summed = [
        (
            lax.psum_scatter(
                self_grads[row_index][1][prefix_count:].astype(jnp.bfloat16),
                "seq",
                scatter_dimension=0,
                tiled=True,
            ).astype(jnp.float32),
            lax.psum_scatter(
                self_grads[row_index][2][prefix_count:].astype(jnp.bfloat16),
                "seq",
                scatter_dimension=0,
                tiled=True,
            ).astype(jnp.float32),
            lax.psum_scatter(
                cross_grads[row_index][1][prefix_count:].astype(jnp.bfloat16),
                "seq",
                scatter_dimension=0,
                tiled=True,
            ).astype(jnp.float32),
            lax.psum_scatter(
                cross_grads[row_index][2][prefix_count:].astype(jnp.bfloat16),
                "seq",
                scatter_dimension=0,
                tiled=True,
            ).astype(jnp.float32),
        )
        for row_index in range(row_count)
    ]
    key_grad = jnp.stack([part[0] for part in summed])
    value_grad = jnp.stack([part[1] for part in summed])
    mkey_grad = jnp.stack([part[2] for part in summed])
    mvalue_grad = jnp.stack([part[3] for part in summed])
    grad_query = jnp.concatenate([part[0] for part in self_grads], 0).astype(low_type)
    d_tokens = (
        grad_one
        + project(grad_query, q_weight.T) * scale
        + project(key_grad.astype(low_type).reshape(-1, width), kv_weight[0].T)
        + project(value_grad.astype(low_type).reshape(-1, width), kv_weight[1].T)
    )
    d_memory = project(mkey_grad.astype(low_type).reshape(-1, width), ckv_weight[0].T) + project(
        mvalue_grad.astype(low_type).reshape(-1, width), ckv_weight[1].T
    )
    totals = lax.psum(
        (pre_self_grad, pre_cross_grad, grad_down_w, grad_down_b, grad_up_w, grad_up_b),
        ("row", "seq"),
    )
    return (
        mixed,
        d_tokens.astype(low_type).reshape(row_count, tok_count, width),
        d_memory.astype(low_type).reshape(row_count, slot_count, width),
        totals[0],
        totals[1],
        totals[2],
        totals[3],
        totals[4],
        totals[5],
    )


def solution(mesh):
    in_specs = (
        P("row", "seq", None),
        P("row", "seq", None),
        P("row"),
        P(),
        P(),
        P(),
        P("row", None),
        P(None, "row", None),
        P("row", None),
        P("row", None),
        P(None, "row", None),
        P("row", None),
        P("row", None),
        P("row", None),
        P(),
        P(),
        P(),
        P(),
        P(),
        P(),
        P("row", "seq", None),
    )
    out_specs = (
        P("row", "seq", None),
        P("row", "seq", None),
        P("row", "seq", None),
        P(),
        P(),
        P(),
        P(),
        P(),
        P(),
    )
    return jax.shard_map(local, mesh=mesh, in_specs=in_specs, out_specs=out_specs, check_vma=False)
```

profile of v0, /device:TPU:0, one launch (start us, length us, event | category | flops | bytes accessed | tf_op | source)
XLA Modules:
  0.0 1328.5 jit_solution(758297019379058807)
XLA Ops:
  13.6 33.9 %all-gather.13.cloned.1.call-done = bf16[2,1024,1024]{2,1,0:T(8,128)(2,1)} async-done(((bf16[2,256,1024]{2,1,0:T(8,128)(2,1)}), bf16[2,1024,1024]{2,1,0:T(8,128)(2,1)}) %all-gather.13.cloned.1.call-update) | async-done | bytes 4194320 | tf_op jit(solution)/shard_map/all_gather | solution.py:119
  55.1 29.0 %all-gather.23.cloned.1.call-done = bf16[2,1024,1024]{2,1,0:T(8,128)(2,1)} async-done(((bf16[2,256,1024]{2,1,0:T(8,128)(2,1)}), bf16[2,1024,1024]{2,1,0:T(8,128)(2,1)}) %all-gather.23.cloned.1.call-update) | async-done | bytes 4194320 | tf_op jit(solution)/shard_map/all_gather | solution.py:122
  110.8 48.9 %all-gather.19.cloned.1.call-done = bf16[2,512,1024]{2,1,0:T(8,128)(2,1)} async-done(((bf16[2,64,1024]{2,1,0:T(8,128)(2,1)}), bf16[2,512,1024]{2,1,0:T(8,128)(2,1)}) %all-gather.19.cloned.1.call-update) | async-done | bytes 2097168 | tf_op jit(solution)/shard_map/all_gather | solution.py:154
  162.9 47.2 %all-gather.15.cloned.1.call-done = bf16[2,512,1024]{2,1,0:T(8,128)(2,1)} async-done(((bf16[2,64,1024]{2,1,0:T(8,128)(2,1)}), bf16[2,512,1024]{2,1,0:T(8,128)(2,1)}) %all-gather.15.cloned.1.call-update) | async-done | bytes 2097168 | tf_op jit(solution)/shard_map/all_gather | solution.py:155
  227.6 5.0 all-gather.21.cloned.1.call-done
  235.3 21.5 %all-gather.27.cloned.1.call-done = bf16[1024,1024]{1,0:T(8,128)(2,1)} async-done(((bf16[256,1024]{1,0:T(8,128)(2,1)}), bf16[1024,1024]{1,0:T(8,128)(2,1)}) %all-gather.27.cloned.1.call-update) | async-done | bytes 2097168 | tf_op jit(solution)/shard_map/all_gather | solution.py:121
  261.8 70.6 %all-gather.29.cloned.1.call-done = bf16[2,1024,1024]{2,1,0:T(8,128)(2,1)} async-done(((bf16[2,128,1024]{2,1,0:T(8,128)(2,1)}), bf16[2,1024,1024]{2,1,0:T(8,128)(2,1)}) %all-gather.29.cloned.1.call-update) | async-done | bytes 4194320 | tf_op jit(solution)/shard_map/all_gather | solution.py:156
  340.9 65.3 %all-gather.25.cloned.1.call-done = bf16[2,1024,1024]{2,1,0:T(8,128)(2,1)} async-done(((bf16[2,128,1024]{2,1,0:T(8,128)(2,1)}), bf16[2,1024,1024]{2,1,0:T(8,128)(2,1)}) %all-gather.25.cloned.1.call-update) | async-done | bytes 4194320 | tf_op jit(solution)/shard_map/all_gather | solution.py:157
  406.2 4.6 fusion.135
  443.0 46.6 %all-gather.33.cloned.1.call-done = bf16[1024,4096]{1,0:T(8,128)(2,1)} async-done(((bf16[256,4096]{1,0:T(8,128)(2,1)}), bf16[1024,4096]{1,0:T(8,128)(2,1)}) %all-gather.33.cloned.1.call-update) | async-done | bytes 8388624 | tf_op jit(solution)/shard_map/all_gather | solution.py:124
  489.6 6.0 fusion.155
  495.6 54.3 %all-gather.35.cloned.1.call-done = bf16[4096,1024]{1,0:T(8,128)(2,1)} async-done(((bf16[1024,1024]{1,0:T(8,128)(2,1)}), bf16[4096,1024]{1,0:T(8,128)(2,1)}) %all-gather.35.cloned.1.call-update) | async-done | bytes 8388624 | tf_op jit(solution)/shard_map/all_gather | solution.py:125
  549.9 10.0 convolution_add_fusion.5
  564.8 17.5 %convolution_add_fusion.4 = f32[128,1024]{1,0:T(8,128)} fusion(f32[128,1024]{1,0:T(8,128)} %copy-done.73, bf16[1024,4096]{1,0:T(8,128)(2,1)} %all-gather.33.cloned.1.call-done, f32[128,4096]{1,0:T(8,128)} %fusion.155, bf16[4096,1024]{1,0:T(8,128)(2,1)} %all-gather.35.cloned.1.call-done), kind=kOutput, calls=%fused_computation.103 | convolution fusion | flops 2185494528 | bytes 19922944 | tf_op jit(solution)/shard_map/dot_general | solution.py:85
  589.8 5.1 multiply_reduce_fusion
  695.7 39.4 %all-reduce.3 = (f32[512]{0:T(512)}, f32[1024]{0:T(1024)}) all-reduce(f32[512]{0:T(512)S(1)} %get-tuple-element.76, f32[1024]{0:T(1024)S(1)} %get-tuple-element.23), channel_id=1, replica_groups=mesh['row'=4,'seq'=8] {'row','seq'}, use_global_device_ids=true, to_apply=%region_36.37 | all-reduce | flops 1536 | bytes 12288 | tf_op jit(solution)/shard_map/psum | solution.py:331
  739.4 8.4 reduce-scatter.15.cloned.1.call-done
  748.7 64.8 %reduce-scatter.9.cloned.1.call-done = bf16[64,1024]{1,0:T(8,128)(2,1)} async-done(((bf16[512,1024]{1,0:T(8,128)(2,1)}), bf16[64,1024]{1,0:T(8,128)(2,1)}) %reduce-scatter.9.cloned.1.call-update) | async-done | bytes 131088 | tf_op jit(solution)/shard_map/reduce_scatter | solution.py:290
  813.6 66.2 %reduce-scatter.11.cloned.1.call-done = bf16[64,1024]{1,0:T(8,128)(2,1)} async-done(((bf16[512,1024]{1,0:T(8,128)(2,1)}), bf16[64,1024]{1,0:T(8,128)(2,1)}) %reduce-scatter.11.cloned.1.call-update) | async-done | bytes 131088 | tf_op jit(solution)/shard_map/reduce_scatter | solution.py:290
  886.3 64.1 %reduce-scatter.23.cloned.1.call-done = bf16[128,1024]{1,0:T(8,128)(2,1)} async-done(((bf16[1024,1024]{1,0:T(8,128)(2,1)}), bf16[128,1024]{1,0:T(8,128)(2,1)}) %reduce-scatter.23.cloned.1.call-update) | async-done | bytes 262160 | tf_op jit(solution)/shard_map/reduce_scatter | solution.py:308
  950.4 70.2 %reduce-scatter.21.cloned.1.call-done = bf16[128,1024]{1,0:T(8,128)(2,1)} async-done(((bf16[1024,1024]{1,0:T(8,128)(2,1)}), bf16[128,1024]{1,0:T(8,128)(2,1)}) %reduce-scatter.21.cloned.1.call-update) | async-done | bytes 262160 | tf_op jit(solution)/shard_map/reduce_scatter | solution.py:308
  1021.7 69.2 %reduce-scatter.19.cloned.1.call-done = bf16[128,1024]{1,0:T(8,128)(2,1)} async-done(((bf16[1024,1024]{1,0:T(8,128)(2,1)}), bf16[128,1024]{1,0:T(8,128)(2,1)}) %reduce-scatter.19.cloned.1.call-update) | async-done | bytes 262160 | tf_op jit(solution)/shard_map/reduce_scatter | solution.py:302
  1091.0 70.8 %reduce-scatter.17.cloned.1.call-done = bf16[128,1024]{1,0:T(8,128)(2,1)} async-done(((bf16[1024,1024]{1,0:T(8,128)(2,1)}), bf16[128,1024]{1,0:T(8,128)(2,1)}) %reduce-scatter.17.cloned.1.call-update) | async-done | bytes 262160 | tf_op jit(solution)/shard_map/reduce_scatter | solution.py:302
  1167.1 146.3 %all-reduce.7.cloned.1.call-done = (f32[2,30,1024]{2,0,1:T(2,128)}, f32[2,30,1024]{2,0,1:T(2,128)}, f32[1024,512]{1,0:T(8,128)}, f32[512,1024]{1,0:T(8,128)}) async-done(((f32[2,30,1024]{2,0,1:T(2,128)}, f32[2,30,1024]{2,0,1:T(2,128)}, f32[1024,512]{1,0:T(8,128)}, f32[512,1024]{1,0:T(8,128)}), (f32[2,30,1024]{2,0,1:T(2,128)}, f32[2,30,1024]{2,0,1:T(2,128)}, f32[1024,512]{1,0:T(8,128)}, ...) | async-done | bytes 4685840 | tf_op jit(solution)/shard_map/psum | solution.py:331
  (390 shorter events, 247.6 us)
Async XLA Ops:
  7.2 40.3 %all-gather.13.cloned.1.call-start = ((), (), s32[]{:S(2)}) async-start(), calls=%async_computation.8 | async-start | bytes 5242880 | tf_op jit(solution)/shard_map/all_gather | solution.py:119
  10.1 74.0 %all-gather.23.cloned.1.call-start = ((), (), s32[]{:S(2)}) async-start(), calls=%async_computation.13 | async-start | bytes 5242880 | tf_op jit(solution)/shard_map/all_gather | solution.py:122
  11.4 97.0 %all-gather.17.cloned.1.call-start = ((), (), s32[]{:S(2)}) async-start(), calls=%async_computation.10 | async-start | bytes 2621440 | tf_op jit(solution)/shard_map/all_gather | solution.py:118
  13.6 146.1 %all-gather.19.cloned.1.call-start = ((), (), s32[]{:S(2)}) async-start(), calls=%async_computation.11 | async-start | bytes 2359296 | tf_op jit(solution)/shard_map/all_gather | solution.py:154
  50.3 159.8 %all-gather.15.cloned.1.call-start = ((), (), s32[]{:S(2)}) async-start(), calls=%async_computation.9 | async-start | bytes 2359296 | tf_op jit(solution)/shard_map/all_gather | solution.py:155
  53.2 179.4 %all-gather.21.cloned.1.call-start = ((), (), s32[]{:S(2)}) async-start(), calls=%async_computation.12 | async-start | bytes 2621440 | tf_op jit(solution)/shard_map/all_gather | solution.py:120
  54.2 202.6 %all-gather.27.cloned.1.call-start = ((), (), s32[]{:S(2)}) async-start(), calls=%async_computation.15 | async-start | bytes 2621440 | tf_op jit(solution)/shard_map/all_gather | solution.py:121
  55.1 277.3 %all-gather.29.cloned.1.call-start = ((), (), s32[]{:S(2)}) async-start(), calls=%async_computation.16 | async-start | bytes 4718592 | tf_op jit(solution)/shard_map/all_gather | solution.py:156
  87.3 318.9 %all-gather.25.cloned.1.call-start = ((), (), s32[]{:S(2)}) async-start(), calls=%async_computation.14 | async-start | bytes 4718592 | tf_op jit(solution)/shard_map/all_gather | solution.py:157
  90.6 347.9 %all-gather.31.cloned.1.call-start = ((), (), s32[]{:S(2)}) async-start(), calls=%async_computation.17 | async-start | bytes 2621440 | tf_op jit(solution)/shard_map/all_gather | solution.py:123
  91.5 398.1 %all-gather.33.cloned.1.call-start = ((), (), s32[]{:S(2)}) async-start(), calls=%async_computation.18 | async-start | bytes 10485760 | tf_op jit(solution)/shard_map/all_gather | solution.py:124
  95.7 454.2 %all-gather.35.cloned.1.call-start = ((), (), s32[]{:S(2)}) async-start(), calls=%async_computation.19 | async-start | bytes 10485760 | tf_op jit(solution)/shard_map/all_gather | solution.py:125
  99.6 639.7 %reduce-scatter.13.cloned.1.call-start = ((), (), s32[]{:S(2)}) async-start(), calls=%async_computation.22 | async-start | bytes 1179648 | tf_op jit(solution)/shard_map/reduce_scatter | solution.py:296
  103.6 116.5 %copy-start.57 = (bf16[1,30,1024]{1,2,0:T(8,128)(2,1)}, bf16[1,30,1024]{1,2,0:T(8,128)(2,1)S(1)}, u32[]{:S(2)}) copy-start(bf16[1,30,1024]{1,2,0:T(8,128)(2,1)S(1)} %copy.64) | copy-start | bytes 184324
  261.7 161.2 %copy-start.46 = (bf16[64,1024]{0,1:T(8,128)(2,1)}, bf16[64,1024]{0,1:T(8,128)(2,1)S(1)}, u32[]{:S(2)}) copy-start(bf16[64,1024]{0,1:T(8,128)(2,1)S(1)} %copy.105) | copy-start | bytes 393220
  617.9 129.9 %reduce-scatter.15.cloned.1.call-start = ((), (), s32[]{:S(2)}) async-start(), calls=%async_computation.23 | async-start | bytes 1179648 | tf_op jit(solution)/shard_map/reduce_scatter | solution.py:296
  627.4 186.2 %reduce-scatter.9.cloned.1.call-start = ((), (), s32[]{:S(2)}) async-start(), calls=%async_computation.20 | async-start | bytes 1179648 | tf_op jit(solution)/shard_map/reduce_scatter | solution.py:290
  638.8 240.9 %reduce-scatter.11.cloned.1.call-start = ((), (), s32[]{:S(2)}) async-start(), calls=%async_computation.21 | async-start | bytes 1179648 | tf_op jit(solution)/shard_map/reduce_scatter | solution.py:290
  642.9 307.5 %reduce-scatter.23.cloned.1.call-start = ((), (), s32[]{:S(2)}) async-start(), calls=%async_computation.27 | async-start | bytes 2359296 | tf_op jit(solution)/shard_map/reduce_scatter | solution.py:308
  651.6 369.0 %reduce-scatter.21.cloned.1.call-start = ((), (), s32[]{:S(2)}) async-start(), calls=%async_computation.26 | async-start | bytes 2359296 | tf_op jit(solution)/shard_map/reduce_scatter | solution.py:308
  664.2 426.8 %reduce-scatter.19.cloned.1.call-start = ((), (), s32[]{:S(2)}) async-start(), calls=%async_computation.25 | async-start | bytes 2359296 | tf_op jit(solution)/shard_map/reduce_scatter | solution.py:302
  674.1 487.6 %reduce-scatter.17.cloned.1.call-start = ((), (), s32[]{:S(2)}) async-start(), calls=%async_computation.24 | async-start | bytes 2359296 | tf_op jit(solution)/shard_map/reduce_scatter | solution.py:302
  680.6 632.7 %all-reduce.7.cloned.1.call-start = ((), (), s32[]{:S(2)}) async-start(), calls=%async_computation.28 | async-start | bytes 9371648 | tf_op jit(solution)/shard_map/psum | solution.py:331
  739.4 143.8 %copy-start.66 = (f32[128,1024]{1,0:T(8,128)S(1)}, f32[128,1024]{1,0:T(8,128)}, u32[]{:S(2)}) copy-start(f32[128,1024]{1,0:T(8,128)} %fusion.33) | copy-start | bytes 1572868
  (89 other events, 776.2 us)
Sparse Core Ops, SparseCore 0:
  10.3 37.1 all-gather.12
  49.6 34.4 all-gather.22
  85.7 22.5 all-gather.16
  110.4 49.2 all-gather.18
  162.3 47.7 all-gather.14
  211.5 21.0 all-gather.20
  234.1 22.5 all-gather.26
  259.0 73.3 all-gather.28
  334.6 71.6 all-gather.24
  408.2 20.8 all-gather.30
  431.3 58.2 all-gather.32
  491.6 58.2 all-gather.34
  618.0 63.5 reduce-scatter.12
  685.2 62.5 reduce-scatter.14
  751.0 62.5 reduce-scatter.8
  817.2 62.4 reduce-scatter.10
  883.7 66.7 reduce-scatter.22
  953.8 66.7 reduce-scatter.20
  1024.2 66.7 reduce-scatter.18
  1094.9 66.7 reduce-scatter.16
  1168.5 144.7 all-reduce.6
where the time goes:
time: 1330 us
  waiting for transfers between devices  984 us (74%)
  matrix products  126 us (9%)
  local copies, waits for them, and re-layouts  123 us (9%)
  blocking collectives  39.4 us (3%)
  other arithmetic  38.3 us (3%)
  between operations  16.1 us (1%)
    psum x1, waiting for transfers between devices, local(): lax.psum((pre_self_grad, pre_cross_grad, grad_down_w, grad_down_b, grad_u...  146 us
    reduce_scatter x2, waiting for transfers between devices, local(): lax.psum_scatter(cross_grads[row_index][1][prefix_count:].astype(jnp.bflo...  140 us
    reduce_scatter x2, waiting for transfers between devices, local(): lax.psum_scatter(cross_grads[row_index][2][prefix_count:].astype(jnp.bflo...  134 us
    reduce_scatter x2, waiting for transfers between devices, local(): lax.psum_scatter(self_grads[row_index][1][prefix_count:].astype(jnp.bfloa...  131 us
    dot_general x23, matrix products, project(): return jnp.dot(left, right, preferred_element_type=jnp.float32)  75.6 us
    all_gather x1, waiting for transfers between devices, local(): lax.all_gather(mem_keys, 'seq', axis=1, tiled=True)  70.6 us
    all_gather x1, waiting for transfers between devices, local(): lax.all_gather(mem_values, 'seq', axis=1, tiled=True)  65.3 us
    all_gather x1, waiting for transfers between devices, local(): lax.all_gather(fc_out.astype(low_type), 'row', axis=0, tiled=True)  54.3 us
  transfers between devices with their start and end apart: 21, of which 19 were waited for; matrix products, arithmetic and copies ran while one was open for 14% of the time, Pallas kernels for 0%

commit v1 on v0

--- a/solution.py
+++ b/solution.py
@@ -36,7 +36,7 @@
 
 
 def head_split(matrix):
-    return matrix.reshape(matrix.shape[0], H, HD)
+    return matrix.reshape(matrix.shape[0], -1, HD)
 
 
 def masked_scores(queries, keys, mask):
@@ -85,7 +85,7 @@
     return jnp.dot(left, right, preferred_element_type=jnp.float32)
 
 
-def local(
+def local_rows(
     tokens,
     memory,
     source_len,
@@ -345,6 +345,231 @@
     )
 
 
+AXES = ("row", "seq")
+
+
+def pairs_of(target):
+    pairs = []
+    for source in range(32):
+        row, seq = divmod(source, 8)
+        x, c, z, y = target(*divmod(row, 2), *divmod(seq, 2))
+        pairs.append((source, (2 * x + c) * 8 + 2 * z + y))
+    return pairs
+
+
+SWAP_X = pairs_of(lambda x, c, z, y: (1 - x, c, z, y))
+SWAP_C = pairs_of(lambda x, c, z, y: (x, 1 - c, z, y))
+SWAP_Y = pairs_of(lambda x, c, z, y: (x, c, z, 1 - y))
+TURN = [pairs_of(lambda x, c, z, y, r=r: (x, z // 2, 2 * c + (z + r) % 2, y)) for r in range(2)]
+
+
+def send(value, pairs):
+    return lax.ppermute(value, AXES, pairs)
+
+
+def turn(first, second, odd):
+    out = [send(jnp.where(odd, second, first), TURN[0]), send(jnp.where(odd, first, second), TURN[1])]
+    return jnp.where(odd, out[1], out[0]), jnp.where(odd, out[0], out[1])
+
+
+def local_pairs(
+    tokens,
+    memory,
+    source_len,
+    bucket_order,
+    prefix_self,
+    prefix_cross,
+    self_query,
+    self_kv,
+    self_out,
+    cross_query,
+    cross_kv,
+    cross_out,
+    fc_in,
+    fc_out,
+    ln_gain,
+    ln_bias,
+    ad_down,
+    ad_down_bias,
+    ad_up,
+    ad_up_bias,
+    cotangent,
+):
+    low = jnp.bfloat16
+    f32 = jnp.float32
+    row, seq = lax.axis_index("row"), lax.axis_index("seq")
+    x, c, z, y = row // 2, row % 2, seq // 2, seq % 2
+    odd = z % 2 == 1
+    scale = HD ** (-0.5)
+    prefix_count = prefix_self.shape[1]
+
+    tok_own = jnp.concatenate(turn(tokens[0], tokens[1], odd), 0)
+    mem_own = jnp.concatenate(turn(memory[0], memory[1], odd), 0)
+    cot_own = jnp.concatenate(turn(cotangent[0], cotangent[1], odd), 0)
+    live = send(jnp.where(odd, source_len[1], source_len[0]).reshape(1, 1), TURN[0])[0, 0]
+    tok_y = send(tok_own, SWAP_Y)
+    tok_c = send(jnp.concatenate([tok_own, tok_y], 0), SWAP_C)
+    tok_all = jnp.concatenate([tok_own, tok_y, tok_c], 0)
+
+    def relative(values):
+        values = jnp.where(c == 0, values, values[::-1])
+        return jnp.where(y == 0, values, values[:, ::-1])
+
+    def by_owner(values, size):
+        values = values.reshape(2, 2, 2, size).transpose(0, 2, 1, 3)
+        return relative(values).reshape(-1)
+
+    places = bucket_order[:, None] * 32 + jnp.arange(32, dtype=jnp.int32)[None]
+    pos = by_owner(places.reshape(-1), 64)
+    slot = by_owner(jnp.arange(1024, dtype=jnp.int32), 128)
+
+    packed = jnp.stack([self_query, self_kv[0], self_kv[1]])
+    packed = lax.dynamic_slice_in_dim(packed.reshape(3, 256, 2, 512), y, 1, 2).reshape(3, 256, 2, 256)
+    packed = packed.astype(low).transpose(2, 0, 1, 3)
+    far = send(packed, SWAP_X)
+    keep, give = jnp.where(c == 0, packed[0], packed[1]), jnp.where(c == 0, packed[1], packed[0])
+    far_keep, far_give = jnp.where(c == 0, far[0], far[1]), jnp.where(c == 0, far[1], far[0])
+    heads_parts = [keep, send(give, SWAP_C), far_keep, send(far_give, SWAP_C)]
+    head_w = jnp.zeros((4, 3, 256, 256), low)
+    for k, part in enumerate(heads_parts):
+        head_w = lax.dynamic_update_index_in_dim(head_w, part, row ^ k, 0)
+    head_w = head_w.transpose(1, 0, 2, 3).reshape(3, 1024, 256)
+
+    def whole(weights):
+        count, rows, cols = weights.shape
+        own = weights.astype(low)
+        half = rows // 2
+        out = lax.dynamic_slice_in_dim(own, y * half, half, 1)
+        x_own = send(out, SWAP_X)
+        x_oth = send(x_own, SWAP_Y)
+        mine = jnp.where(y == 0, jnp.concatenate([x_own, x_oth], 1), jnp.concatenate([x_oth, x_own], 1))
+        full = jnp.zeros((count, 4, rows, cols), low)
+        full = lax.dynamic_update_index_in_dim(full, own, row, 1)
+        full = lax.dynamic_update_index_in_dim(full, send(own, SWAP_C), row ^ 1, 1)
+        full = lax.dynamic_update_index_in_dim(full, mine, row ^ 2, 1)
+        full = lax.dynamic_update_index_in_dim(full, send(mine, SWAP_C), row ^ 3, 1)
+        return full.reshape(count, 4 * rows, cols)
+
+    ckv_weight = whole(cross_kv)
+    mid = whole(jnp.stack([self_out, cross_query, cross_out]))
+    o_weight, cq_weight, co_weight = mid[0], mid[1], mid[2]
+    in_weight = whole(fc_in[None])[0]
+    out_weight = whole(fc_out[None])[0]
+
+    mk = project(mem_own, ckv_weight[0]).astype(low)
+    mv = project(mem_own, ckv_weight[1]).astype(low)
+    mkv = jnp.stack([mk, mv])
+    mkv_y = send(mkv, SWAP_Y)
+    mkv2 = jnp.concatenate([mkv, mkv_y], 1)
+    mkv_c = send(mkv2, SWAP_C)
+    pre_cross = prefix_cross.astype(low)
+    cross_k = jnp.concatenate([pre_cross[0], mkv2[0], mkv_c[0]], 0)
+    cross_v = jnp.concatenate([pre_cross[1], mkv2[1], mkv_c[1]], 0)
+    cross_mask = jnp.concatenate([jnp.ones((prefix_count,), jnp.bool_), slot < live])[None, :]
+
+    group = 2 * y + c
+    q = (project(tok_all, head_w[0]) * scale).astype(low)
+    k = project(tok_all, head_w[1]).astype(low)
+    v = project(tok_all, head_w[2]).astype(low)
+    pre = lax.dynamic_slice_in_dim(prefix_self, group * 256, 256, 2).astype(low)
+    self_k = jnp.concatenate([pre[0], k], 0)
+    self_v = jnp.concatenate([pre[1], v], 0)
+    self_mask = jnp.concatenate(
+        [jnp.ones((512, prefix_count), jnp.bool_), pos[None, :] <= pos[:, None]], axis=1
+    )
+    att, self_lse = attend(q, self_k, self_v, self_mask)
+    att = att.astype(low)
+
+    def natural(parts):
+        full = jnp.zeros((4, 128, 256), low)
+        for k, part in enumerate(parts):
+            where = (2 * (y ^ (k & 1))) + (c ^ (k >> 1))
+            full = lax.dynamic_update_index_in_dim(full, part, where, 0)
+        return full.transpose(1, 0, 2).reshape(128, 1024)
+
+    att = att.reshape(4, 128, 256)
+    got = send(jnp.stack([att[1], att[3]]), SWAP_Y)
+    got_c = send(jnp.stack([att[2], got[1]]), SWAP_C)
+    attended = natural([att[0], got[0], got_c[0], got_c[1]])
+
+    resid_one = tok_own.astype(f32) + project(attended, o_weight)
+    hidden_one, unit_one, inv_one = normalize(resid_one, ln_gain[0], ln_bias[0])
+    cq = (project(hidden_one.astype(low), cq_weight) * scale).astype(low)
+    catt, cross_lse = attend(cq, cross_k, cross_v, cross_mask)
+    resid_two = hidden_one + project(catt.astype(low), co_weight)
+    hidden_two, unit_two, inv_two = normalize(resid_two, ln_gain[1], ln_bias[1])
+    hidden_low = hidden_two.astype(low)
+    up_proj = project(hidden_low, in_weight)
+    activated = gelu_exact(up_proj).astype(low)
+    ffn_out = project(activated, out_weight)
+    down_weight = ad_down.astype(low)
+    up_weight = ad_up.astype(low)
+    down_proj = project(hidden_low, down_weight) + ad_down_bias
+    down_act = gelu_exact(down_proj).astype(low)
+    adapted = project(down_act, up_weight) + ad_up_bias
+    resid_three = hidden_two + ffn_out + 4.0 * adapted
+    output, unit_three, inv_three = normalize(resid_three, ln_gain[2], ln_bias[2])
+    mixed = output.astype(low).reshape(2, 64, 1024)
+    mixed = jnp.stack(turn(mixed[0], mixed[1], odd))
+
+    grad_three = normalize_back(cot_own.astype(f32), unit_three, inv_three, ln_gain[2])
+    grad_ffn = grad_three.astype(low)
+    grad_adapt = (4.0 * grad_three).astype(low)
+    grad_up_w = jnp.einsum("na,nd->ad", down_act, grad_adapt, preferred_element_type=f32)
+    grad_up_b = jnp.sum(grad_adapt.astype(f32), axis=0)
+    grad_down = gelu_back(down_proj, project(grad_adapt, up_weight.T)).astype(low)
+    grad_down_w = jnp.einsum("nd,na->da", hidden_low, grad_down, preferred_element_type=f32)
+    grad_down_b = jnp.sum(grad_down.astype(f32), axis=0)
+    grad_inner = gelu_back(up_proj, project(grad_ffn, out_weight.T)).astype(low)
+    grad_hidden_two = (
+        grad_three + project(grad_inner, in_weight.T) + project(grad_down, down_weight.T)
+    )
+    grad_two = normalize_back(grad_hidden_two, unit_two, inv_two, ln_gain[1])
+    grad_catt = project(grad_two.astype(low), co_weight.T).astype(low)
+    grad_cq, grad_ck, grad_cv = attend_back(cq, cross_k, cross_v, cross_mask, cross_lse, grad_catt)
+    grad_hidden_one = grad_two + project(grad_cq.astype(low), cq_weight.T) * scale
+    grad_one = normalize_back(grad_hidden_one, unit_one, inv_one, ln_gain[0])
+    grad_att = project(grad_one.astype(low), o_weight.T).astype(low)
+
+    parts = grad_att.reshape(128, 4, 256)
+    at = lambda k: lax.dynamic_index_in_dim(
+        parts, (2 * (y ^ (k & 1))) + (c ^ (k >> 1)), 1, keepdims=False
+    )
+    got_c = send(jnp.stack([at(2), at(3)]), SWAP_C)
+    got = send(jnp.stack([at(1), got_c[1]]), SWAP_Y)
+    grad_o = jnp.concatenate([at(0), got[0], got_c[0], got[1]], 0)
+    dq, dk, dv = attend_back(q, self_k, self_v, self_mask, self_lse, grad_o)
+
+    def fold(values):
+        half = send(values[2:].astype(low), SWAP_C).astype(f32) + values[:2]
+        return half[0] + send(half[1].astype(low), SWAP_Y).astype(f32)
+
+    dmkv = jnp.concatenate([grad_ck[prefix_count:], grad_cv[prefix_count:]], 1).reshape(4, 256, 2048)
+    dmkv = fold(dmkv).astype(low)
+    d_memory = project(dmkv[:, :1024], ckv_weight[0].T) + project(dmkv[:, 1024:], ckv_weight[1].T)
+    d_memory = d_memory.astype(low).reshape(2, 128, 1024)
+    d_memory = jnp.stack(turn(d_memory[0], d_memory[1], odd))
+
+    part = (
+        project(dq.astype(low), head_w[0].T) * scale
+        + project(dk[prefix_count:].astype(low), head_w[1].T)
+        + project(dv[prefix_count:].astype(low), head_w[2].T)
+    )
+    d_tokens = (grad_one + fold(part.reshape(4, 128, 1024))).astype(low).reshape(2, 64, 1024)
+    d_tokens = jnp.stack(turn(d_tokens[0], d_tokens[1], odd))
+
+    pre_self_grad = jnp.stack([dk[:prefix_count], dv[:prefix_count]])
+    pre_self_grad = lax.dynamic_update_slice_in_dim(
+        jnp.zeros(prefix_self.shape, f32), pre_self_grad, group * 256, 2
+    )
+    pre_cross_grad = jnp.stack([grad_ck[:prefix_count], grad_cv[:prefix_count]])
+    totals = lax.psum(
+        (pre_self_grad, pre_cross_grad, grad_down_w, grad_down_b, grad_up_w, grad_up_b),
+        ("row", "seq"),
+    )
+    return (mixed, d_tokens, d_memory, *totals)
+
+
 def solution(mesh):
     in_specs = (
         P("row", "seq", None),
@@ -380,4 +605,5 @@
         P(),
         P(),
     )
+    local = local_pairs if (mesh.shape["row"], mesh.shape["seq"]) == (4, 8) else local_rows
     return jax.shard_map(local, mesh=mesh, in_specs=in_specs, out_specs=out_specs, check_vma=False)

time: 1330 us -> 631 us (0.47)
  waiting for transfers between devices: 984 us -> 218 us
  starting transfers between devices: 1.34 us -> 60 us
  matrix products: 126 us -> 90.7 us
  other arithmetic: 38.3 us -> 71.5 us
    all_gather x12 -> x0, waiting for transfers between devices: 424 us -> none  [the longest x1 70.6 us: local(): lax.all_gather(mem_keys, 'seq', axis=1, tiled=True)]
    reduce_scatter x8 -> x0, waiting for transfers between devices: 414 us -> none  [the longest x2 140 us: local(): lax.psum_scatter(cross_grads[row_index][1][prefix_count:].astype(jnp.bflo...]
    ppermute x0 -> x44, waiting for transfers between devices: none -> 122 us  [send(): return lax.ppermute(value, AXES, pairs)]
    ppermute x0 -> x44, starting transfers between devices: none -> 60 us  [send(): return lax.ppermute(value, AXES, pairs)]
    psum x1, waiting for transfers between devices: 146 us -> 95.7 us  [local_pairs(): lax.psum((pre_self_grad, pre_cross_grad, grad_down_w, grad_down_b, grad_u...]
    dot_general x23, matrix products: 75.6 us -> 44 us  [project(): return jnp.dot(left, right, preferred_element_type=jnp.float32)]
    dynamic_update_slice x0 -> x15, local copies, waits for them, and re-layouts: none -> 19.5 us  [the longest x4 10.2 us: whole(): full = lax.dynamic_update_index_in_dim(full, send(mine, SWAP_C), row ^ 3, 1)]
    select_n x0 -> x17, other arithmetic: none -> 19.4 us  [the longest x4 8.45 us: whole(): jnp.where(y == 0, jnp.concatenate([x_own, x_oth], 1), jnp.concatenate([x_...]
  transfers between devices with their start and end apart: 21 -> 45, of which waited for: 19 -> 13; matrix products, arithmetic and copies ran while one was open for 14% -> 26% of each run, Pallas kernels for 0% -> 0%
where the time goes in v1:
time: 631 us; the launch traced here: 623 us
  waiting for transfers between devices  218 us (35%)
  local copies, waits for them, and re-layouts  127 us (20%)
  matrix products  90.7 us (14%)
  other arithmetic  71.5 us (11%)
  starting transfers between devices  60 us (10%)
  blocking collectives  38.9 us (6%)
  between operations  17.5 us (3%)
    ppermute x44, waiting for transfers between devices, send(): return lax.ppermute(value, AXES, pairs)  122 us
    psum x1, waiting for transfers between devices, local_pairs(): lax.psum((pre_self_grad, pre_cross_grad, grad_down_w, grad_down_b, grad_u...  95.7 us
    ppermute x44, starting transfers between devices, send(): return lax.ppermute(value, AXES, pairs)  60 us
    dot_general x23, matrix products, project(): return jnp.dot(left, right, preferred_element_type=jnp.float32)  44 us
    psum x1, blocking collectives, local_pairs(): lax.psum((pre_self_grad, pre_cross_grad, grad_down_w, grad_down_b, grad_u...  38.9 us
    unnamed x223, local copies, waits for them, and re-layouts  27.2 us
    dot_general x2, matrix products, attend_back(): jnp.einsum('qhd,khd->hqk', grad_heads, head_split(values), preferred_elem...  13 us
  transfers between devices with their start and end apart: 45, of which 13 were waited for; matrix products, arithmetic and copies ran while one was open for 26% of the time, Pallas kernels for 0%

profile of v1, /device:TPU:0, one launch (start us, length us, event | category | flops | bytes accessed | tf_op | source)
XLA Modules:
  0.0 623.5 jit_solution(13422917726978550204)
XLA Ops:
  23.8 6.0 collective-permute-start.15
  46.9 4.4 broadcast_in_dim.151
  75.4 4.4 collective-permute-start.9
  107.1 8.0 %collective-permute-done.16 = bf16[2,128,1024]{2,1,0:T(8,128)(2,1)S(1)} collective-permute-done((bf16[2,128,1024]{2,1,0:T(8,128)(2,1)}, bf16[2,128,1024]{2,1,0:T(8,128)(2,1)S(1)}, u32[]{:S(2)}, u32[]{:S(2)}) %collective-permute-start.16) | collective-permute-done | bytes 524320 | tf_op jit(solution)/shard_map/ppermute | solution.py:367
  124.8 4.1 collective-permute-done.17
  131.9 16.6 %collective-permute-done.7 = bf16[2,128,256]{1,2,0:T(8,128)(2,1)S(1)} collective-permute-done((bf16[2,128,256]{1,2,0:T(8,128)(2,1)S(1)}, bf16[2,128,256]{1,2,0:T(8,128)(2,1)S(1)}, u32[]{:S(2)}, u32[]{:S(2)}) %collective-permute-start.7) | collective-permute-done | bytes 131104 | tf_op jit(solution)/shard_map/ppermute | solution.py:367
  175.7 9.7 %collective-permute-done.28 = bf16[1,512,1024]{2,1,0:T(8,128)(2,1)S(1)} collective-permute-done((bf16[1,512,1024]{2,1,0:T(8,128)(2,1)S(1)}, bf16[1,512,1024]{2,1,0:T(8,128)(2,1)S(1)}, u32[]{:S(2)}, u32[]{:S(2)}) %collective-permute-start.28) | collective-permute-done | bytes 1048608 | tf_op jit(solution)/shard_map/ppermute | solution.py:367
  189.7 18.2 %collective-permute-done.24 = bf16[1,128,4096]{2,1,0:T(8,128)(2,1)S(1)} collective-permute-done((bf16[1,128,4096]{2,1,0:T(8,128)(2,1)S(1)}, bf16[1,128,4096]{2,1,0:T(8,128)(2,1)S(1)}, u32[]{:S(2)}, u32[]{:S(2)}) %collective-permute-start.24) | collective-permute-done | bytes 1048608 | tf_op jit(solution)/shard_map/ppermute | solution.py:367
  218.7 11.7 %collective-permute-done.19 = bf16[2,256,1024]{2,1,0:T(8,128)(2,1)S(1)} collective-permute-done((bf16[2,256,1024]{2,1,0:T(8,128)(2,1)S(1)}, bf16[2,256,1024]{2,1,0:T(8,128)(2,1)S(1)}, u32[]{:S(2)}, u32[]{:S(2)}) %collective-permute-start.19) | collective-permute-done | bytes 1048608 | tf_op jit(solution)/shard_map/ppermute | solution.py:367
  239.9 4.9 fusion.99
  260.2 4.7 concatenate.262
  270.2 5.0 concatenate.257
  275.2 6.0 convolution_convert_fusion.6
  282.1 5.3 fusion.121
  290.7 5.6 fusion.115
  300.7 17.3 %fusion.98 = (f32[128]{0:T(128)S(1)}, f32[128]{0:T(128)S(1)}, f32[128,1024]{1,0:T(8,128)S(1)}) fusion(f32[128]{0:T(128)S(1)} %add_rsqrt_fusion.1, f32[128,1024]{1,0:T(8,128)S(1)} %get-tuple-element.109, f32[128]{0:T(128)S(1)} %broadcast_multiply_fusion.7, f32[1024]{0:T(1024)S(1)} %bitcast.340, f32[128,1024]{1,0:T(8,128)} %fusion.48, ...), kind=kOutput, calls=%fused_computation.291 | convolution fusion | flops 2186412032 | bytes 20977664 | tf_op jit(solution)/shard_map/dot_general | solution.py:85
  320.8 7.4 %convolution_bitcast_fusion = f32[1054,16,64]{0,2,1:T(8,128)} fusion(bf16[128,16,64]{0,2,1:T(8,128)(2,1)S(1)} %bitcast.285, f32[16,128,1054]{1,2,0:T(8,128)} %copy-done.2, f32[16,128]{1,0:T(8,128)S(1)} %log_add_fusion), kind=kOutput, calls=%fused_computation.12 | convolution fusion | flops 280616960 | bytes 13221888 | tf_op jit(solution)/shard_map/hqk,qhd->khd/dot_general | solution.py:74
  328.2 9.1 %multiply_reduce_fusion = (f32[16,128]{1,0:T(8,128)S(1)}, f32[16,128,1054]{1,2,0:T(8,128)}) fusion(f32[16,128,1054]{1,2,0:T(8,128)} %copy-done.2, f32[16,128]{1,0:T(8,128)S(1)} %log_add_fusion, bf16[128,16,64]{0,2,1:T(8,128)(2,1)S(1)} %bitcast.286, bf16[1054,16,64]{0,2,1:T(8,128)(2,1)S(1)} %copy-done.9), kind=kOutput, calls=%fused_computation.1 | convolution fusion | flops 282773504 | bytes 19705856 | tf_op jit(solution)/shard_map/qhd,khd->hqk/dot_general | solution.py:63
  337.3 7.7 %multiply_convert_fusion = bf16[16,128,1054]{1,2,0:T(8,128)(2,1)S(1)} fusion(f32[16,128,1054]{1,2,0:T(8,128)} %get-tuple-element.114, f32[16,128,1054]{1,2,0:T(8,128)} %copy-done.2, f32[16,128]{1,0:T(8,128)S(1)} %get-tuple-element.113, f32[16,128]{1,0:T(8,128)S(1)} %log_add_fusion), kind=kLoop, calls=%fused_computation | loop fusion | flops 8634368 | bytes 21602304 | tf_op jit(solution)/shard_map/convert_element_type | solution.py:67
  377.3 5.5 copy.110
  385.9 38.9 %all-reduce.2 = (f32[512]{0:T(512)}, f32[1024]{0:T(1024)}) all-reduce(f32[512]{0:T(512)S(1)} %get-tuple-element.118, f32[1024]{0:T(1024)S(1)} %get-tuple-element.21), channel_id=1, replica_groups=mesh['row'=4,'seq'=8] {'row','seq'}, use_global_device_ids=true, to_apply=%region_22.23 | all-reduce | flops 1536 | bytes 12288 | tf_op jit(solution)/shard_map/psum | solution.py:566
  456.8 35.2 %collective-permute-done.37 = bf16[128,1024]{1,0:T(8,128)(2,1)} collective-permute-done((bf16[128,1024]{1,0:T(8,128)(2,1)}, bf16[128,1024]{1,0:T(8,128)(2,1)}, u32[]{:S(2)}, u32[]{:S(2)}) %collective-permute-start.37) | collective-permute-done | bytes 262176 | tf_op jit(solution)/shard_map/ppermute | solution.py:367
  502.1 9.9 %collective-permute-done.42 = bf16[128,1024]{1,0:T(8,128)(2,1)S(1)} collective-permute-done((bf16[128,1024]{1,0:T(8,128)(2,1)S(1)}, bf16[128,1024]{1,0:T(8,128)(2,1)S(1)}, u32[]{:S(2)}, u32[]{:S(2)}) %collective-permute-start.42) | collective-permute-done | bytes 262176 | tf_op jit(solution)/shard_map/ppermute | solution.py:367
  512.9 95.7 %all-reduce.6.cloned.1.call-done = (f32[2,30,1024]{2,0,1:T(2,128)}, f32[2,30,1024]{2,0,1:T(2,128)}, f32[1024,512]{1,0:T(8,128)}, f32[512,1024]{1,0:T(8,128)}) async-done(((f32[2,30,1024]{2,0,1:T(2,128)}, f32[2,30,1024]{2,0,1:T(2,128)}, f32[1024,512]{1,0:T(8,128)}, f32[512,1024]{1,0:T(8,128)}), (f32[2,30,1024]{2,0,1:T(2,128)}, f32[2,30,1024]{2,0,1:T(2,128)}, f32[1024,512]{1,0:T(8,128)}, ...) | async-done | bytes 4685840 | tf_op jit(solution)/shard_map/psum | solution.py:566
  (504 shorter events, 264.7 us)
Async XLA Ops:
  7.2 601.4 %all-reduce.6.cloned.1.call-start = ((), (), s32[]{:S(2)}) async-start(), calls=%async_computation | async-start | bytes 9371648 | tf_op jit(solution)/shard_map/psum | solution.py:566
  9.9 55.2 %collective-permute-start.21 = (s32[1,1]{1,0:T(1,128)}, s32[1,1]{1,0:T(1,128)}, u32[]{:S(2)}, u32[]{:S(2)}) collective-permute-start(s32[1,1]{1,0:T(1,128)} %bitcast.60), channel_id=1, source_target_pairs={{0,0},{1,1},{2,2},{3,3},{4,8},{5,9},{6,10},{7,11},{8,4},{9,5},{10,... | collective-permute-start | bytes 20 | tf_op jit(solution)/shard_map/ppermute | solution.py:367
  12.7 54.3 %collective-permute-start = (bf16[64,1024]{1,0:T(8,128)(2,1)}, bf16[64,1024]{1,0:T(8,128)(2,1)}, u32[]{:S(2)}, u32[]{:S(2)}) collective-permute-start(bf16[64,1024]{1,0:T(8,128)(2,1)} %get-tuple-element.82), channel_id=1, source_target_pairs={{0,2},{1,3},{2,0},{3,1},{4,10},{5,11},{6,8},{7,9},{8,6},{9,7},{10,... | collective-permute-start | bytes 393224 | tf_op jit(solution)/shard_map/ppermute | solution.py:367
  15.8 52.5 %collective-permute-start.1 = (bf16[64,1024]{1,0:T(8,128)(2,1)}, bf16[64,1024]{1,0:T(8,128)(2,1)}, u32[]{:S(2)}, u32[]{:S(2)}) collective-permute-start(bf16[64,1024]{1,0:T(8,128)(2,1)} %get-tuple-element.83), channel_id=1, source_target_pairs={{0,0},{1,1},{2,2},{3,3},{4,8},{5,9},{6,10},{7,11},{8,4},{9,5},{10,... | collective-permute-start | bytes 393224 | tf_op jit(solution)/shard_map/ppermute | solution.py:367
  19.6 51.2 %collective-permute-start.32 = (bf16[64,1024]{1,0:T(8,128)(2,1)}, bf16[64,1024]{1,0:T(8,128)(2,1)}, u32[]{:S(2)}, u32[]{:S(2)}) collective-permute-start(bf16[64,1024]{1,0:T(8,128)(2,1)} %get-tuple-element.70), channel_id=1, source_target_pairs={{0,2},{1,3},{2,0},{3,1},{4,10},{5,11},{6,8},{7,9},{8,6},{9,7},{10,... | collective-permute-start | bytes 393224 | tf_op jit(solution)/shard_map/ppermute | solution.py:367
  23.8 78.6 %collective-permute-start.15 = (bf16[2,256,1024]{2,1,0:T(8,128)(2,1)}, bf16[2,256,1024]{2,1,0:T(8,128)(2,1)}, u32[]{:S(2)}, u32[]{:S(2)}) collective-permute-start(bf16[2,256,1024]{2,1,0:T(8,128)(2,1)} %get-tuple-element.28), channel_id=1, source_target_pairs={{0,8},{1,9},{2,10},{3,11},{4,12},{5,13},{6,14},{7,15},{8,0},{9,1},... | collective-permute-start | bytes 3145736 | tf_op jit(solution)/shard_map/ppermute | solution.py:367
  75.4 77.4 %collective-permute-start.9 = (bf16[3,256,1024]{2,1,0:T(8,128)(2,1)}, bf16[3,256,1024]{2,1,0:T(8,128)(2,1)}, u32[]{:S(2)}, u32[]{:S(2)}) collective-permute-start(bf16[3,256,1024]{2,1,0:T(8,128)(2,1)} %copy-done.38), channel_id=1, source_target_pairs={{0,8},{1,9},{2,10},{3,11},{4,12},{5,13},{6,14},{7,15},{8,0},{9,1},... | collective-permute-start | bytes 4718600 | tf_op jit(solution)/shard_map/ppermute | solution.py:367
  79.8 36.9 %collective-permute-start.10 = (bf16[3,128,1024]{2,1,0:T(8,128)(2,1)}, bf16[3,128,1024]{2,1,0:T(8,128)(2,1)}, u32[]{:S(2)}, u32[]{:S(2)}) collective-permute-start(bf16[3,128,1024]{2,1,0:T(8,128)(2,1)} %constant_dynamic-slice_fusion.5), channel_id=1, source_target_pairs={{0,16},{1,17},{2,18},{3,19},{4,20},{5,21},{6,22},{7,23},{8,24},{9,... | collective-permute-start | bytes 2359304 | tf_op jit(solution)/shard_map/ppermute | solution.py:367
  105.4 50.3 %collective-permute-start.27 = (bf16[1,512,1024]{2,1,0:T(8,128)(2,1)S(1)}, bf16[1,512,1024]{2,1,0:T(8,128)(2,1)S(1)}, u32[]{:S(2)}, u32[]{:S(2)}) collective-permute-start(bf16[1,512,1024]{2,1,0:T(8,128)(2,1)S(1)} %copy-done.61), channel_id=1, source_target_pairs={{0,16},{1,17},{2,18},{3,19},{4,20},{5,21},{6,22},{7,23},{8,24},{9,... | collective-permute-start | bytes 3145736 | tf_op jit(solution)/shard_map/ppermute | solution.py:367
  115.1 44.9 %collective-permute-start.23 = (bf16[1,128,4096]{2,1,0:T(8,128)(2,1)S(1)}, bf16[1,128,4096]{2,1,0:T(8,128)(2,1)S(1)}, u32[]{:S(2)}, u32[]{:S(2)}) collective-permute-start(bf16[1,128,4096]{2,1,0:T(8,128)(2,1)S(1)} %copy-done.60), channel_id=1, source_target_pairs={{0,16},{1,17},{2,18},{3,19},{4,20},{5,21},{6,22},{7,23},{8,24},{9,... | collective-permute-start | bytes 3145736 | tf_op jit(solution)/shard_map/ppermute | solution.py:367
  118.2 43.4 %collective-permute-start.11 = (bf16[3,128,1024]{2,1,0:T(8,128)(2,1)}, bf16[3,128,1024]{2,1,0:T(8,128)(2,1)S(1)}, u32[]{:S(2)}, u32[]{:S(2)}) collective-permute-start(bf16[3,128,1024]{2,1,0:T(8,128)(2,1)} %collective-permute-done.10), channel_id=1, source_target_pairs={{0,1},{1,0},{2,3},{3,2},{4,5},{5,4},{6,7},{7,6},{8,9},{9,8},{10,11... | collective-permute-start | bytes 2359304 | tf_op jit(solution)/shard_map/ppermute | solution.py:367
  152.8 60.1 %collective-permute-start.26 = (bf16[1,1024,1024]{2,1,0:T(8,128)(2,1)S(1)}, bf16[1,1024,1024]{2,1,0:T(8,128)(2,1)S(1)}, u32[]{:S(2)}, u32[]{:S(2)}) collective-permute-start(bf16[1,1024,1024]{2,1,0:T(8,128)(2,1)S(1)} %bitcast.271), channel_id=1, source_target_pairs={{0,8},{1,9},{2,10},{3,11},{4,12},{5,13},{6,14},{7,15},{8,0},{9,1},... | collective-permute-start | bytes 6291464 | tf_op jit(solution)/shard_map/ppermute | solution.py:367
  155.7 55.6 %collective-permute-start.22 = (bf16[1,256,4096]{2,1,0:T(8,128)(2,1)S(1)}, bf16[1,256,4096]{2,1,0:T(8,128)(2,1)S(1)}, u32[]{:S(2)}, u32[]{:S(2)}) collective-permute-start(bf16[1,256,4096]{2,1,0:T(8,128)(2,1)S(1)} %bitcast.270), channel_id=1, source_target_pairs={{0,8},{1,9},{2,10},{3,11},{4,12},{5,13},{6,14},{7,15},{8,0},{9,1},... | collective-permute-start | bytes 6291464 | tf_op jit(solution)/shard_map/ppermute | solution.py:367
  161.6 46.3 %collective-permute-start.24 = (bf16[1,128,4096]{2,1,0:T(8,128)(2,1)S(1)}, bf16[1,128,4096]{2,1,0:T(8,128)(2,1)S(1)}, u32[]{:S(2)}, u32[]{:S(2)}) collective-permute-start(bf16[1,128,4096]{2,1,0:T(8,128)(2,1)S(1)} %collective-permute-done.23), channel_id=1, source_target_pairs={{0,1},{1,0},{2,3},{3,2},{4,5},{5,4},{6,7},{7,6},{8,9},{9,8},{10,11... | collective-permute-start | bytes 3145736 | tf_op jit(solution)/shard_map/ppermute | solution.py:367
  168.7 68.4 %collective-permute-start.12 = (bf16[3,256,1024]{2,1,0:T(8,128)(2,1)}, bf16[3,256,1024]{2,1,0:T(8,128)(2,1)}, u32[]{:S(2)}, u32[]{:S(2)}) collective-permute-start(bf16[3,256,1024]{2,1,0:T(8,128)(2,1)} %maximum_select_fusion.5), channel_id=1, source_target_pairs={{0,8},{1,9},{2,10},{3,11},{4,12},{5,13},{6,14},{7,15},{8,0},{9,1},... | collective-permute-start | bytes 4718600 | tf_op jit(solution)/shard_map/ppermute | solution.py:367
  185.4 44.9 %collective-permute-start.19 = (bf16[2,256,1024]{2,1,0:T(8,128)(2,1)S(1)}, bf16[2,256,1024]{2,1,0:T(8,128)(2,1)S(1)}, u32[]{:S(2)}, u32[]{:S(2)}) collective-permute-start(bf16[2,256,1024]{2,1,0:T(8,128)(2,1)S(1)} %pad_maximum_fusion.4), channel_id=1, source_target_pairs={{0,1},{1,0},{2,3},{3,2},{4,5},{5,4},{6,7},{7,6},{8,9},{9,8},{10,11... | collective-permute-start | bytes 3145736 | tf_op jit(solution)/shard_map/ppermute | solution.py:367
  207.9 41.5 %collective-permute-start.29 = (bf16[1,1024,1024]{2,1,0:T(8,128)(2,1)}, bf16[1,1024,1024]{2,1,0:T(8,128)(2,1)}, u32[]{:S(2)}, u32[]{:S(2)}) collective-permute-start(bf16[1,1024,1024]{2,1,0:T(8,128)(2,1)} %maximum_select_fusion.3), channel_id=1, source_target_pairs={{0,8},{1,9},{2,10},{3,11},{4,12},{5,13},{6,14},{7,15},{8,0},{9,1},... | collective-permute-start | bytes 6291464 | tf_op jit(solution)/shard_map/ppermute | solution.py:367
  211.3 41.3 %collective-permute-start.25 = (bf16[1,256,4096]{2,1,0:T(8,128)(2,1)}, bf16[1,256,4096]{2,1,0:T(8,128)(2,1)}, u32[]{:S(2)}, u32[]{:S(2)}) collective-permute-start(bf16[1,256,4096]{2,1,0:T(8,128)(2,1)} %maximum_select_fusion.1), channel_id=1, source_target_pairs={{0,8},{1,9},{2,10},{3,11},{4,12},{5,13},{6,14},{7,15},{8,0},{9,1},... | collective-permute-start | bytes 6291464 | tf_op jit(solution)/shard_map/ppermute | solution.py:367
  368.9 57.9 %collective-permute-start.35 = (bf16[2,128,256]{2,1,0:T(8,128)(2,1)}, bf16[2,128,256]{2,1,0:T(8,128)(2,1)}, u32[]{:S(2)}, u32[]{:S(2)}) collective-permute-start(bf16[2,128,256]{2,1,0:T(8,128)(2,1)} %pad_maximum_fusion.25), channel_id=1, source_target_pairs={{0,1},{1,0},{2,3},{3,2},{4,5},{5,4},{6,7},{7,6},{8,9},{9,8},{10,11... | collective-permute-start | bytes 393224 | tf_op jit(solution)/shard_map/ppermute | solution.py:367
  371.1 82.8 %collective-permute-start.30 = (bf16[64,1024]{1,0:T(8,128)(2,1)}, bf16[64,1024]{1,0:T(8,128)(2,1)}, u32[]{:S(2)}, u32[]{:S(2)}) collective-permute-start(bf16[64,1024]{1,0:T(8,128)(2,1)} %get-tuple-element.74), channel_id=1, source_target_pairs={{0,2},{1,3},{2,0},{3,1},{4,10},{5,11},{6,8},{7,9},{8,6},{9,7},{10,... | collective-permute-start | bytes 393224 | tf_op jit(solution)/shard_map/ppermute | solution.py:367
  373.3 80.7 %collective-permute-start.31 = (bf16[64,1024]{1,0:T(8,128)(2,1)}, bf16[64,1024]{1,0:T(8,128)(2,1)}, u32[]{:S(2)}, u32[]{:S(2)}) collective-permute-start(bf16[64,1024]{1,0:T(8,128)(2,1)} %get-tuple-element.75), channel_id=1, source_target_pairs={{0,0},{1,1},{2,2},{3,3},{4,8},{5,9},{6,10},{7,11},{8,4},{9,5},{10,... | collective-permute-start | bytes 393224 | tf_op jit(solution)/shard_map/ppermute | solution.py:367
  385.2 60.7 %collective-permute-start.40 = (bf16[2,256,2048]{2,1,0:T(8,128)(2,1)}, bf16[2,256,2048]{2,1,0:T(8,128)(2,1)}, u32[]{:S(2)}, u32[]{:S(2)}) collective-permute-start(bf16[2,256,2048]{2,1,0:T(8,128)(2,1)} %bitcast.290), channel_id=1, source_target_pairs={{0,8},{1,9},{2,10},{3,11},{4,12},{5,13},{6,14},{7,15},{8,0},{9,1},... | collective-permute-start | bytes 6291464 | tf_op jit(solution)/shard_map/ppermute | solution.py:367
  450.4 44.6 %collective-permute-start.41 = (bf16[256,2048]{1,0:T(8,128)(2,1)S(1)}, bf16[256,2048]{1,0:T(8,128)(2,1)}, u32[]{:S(2)}, u32[]{:S(2)}) collective-permute-start(bf16[256,2048]{1,0:T(8,128)(2,1)S(1)} %fusion.32), channel_id=1, source_target_pairs={{0,1},{1,0},{2,3},{3,2},{4,5},{5,4},{6,7},{7,6},{8,9},{9,8},{10,11... | collective-permute-start | bytes 3145736 | tf_op jit(solution)/shard_map/ppermute | solution.py:367
  453.7 38.2 %collective-permute-start.37 = (bf16[128,1024]{1,0:T(8,128)(2,1)}, bf16[128,1024]{1,0:T(8,128)(2,1)}, u32[]{:S(2)}, u32[]{:S(2)}) collective-permute-start(bf16[128,1024]{1,0:T(8,128)(2,1)} %fusion.55), channel_id=1, source_target_pairs={{0,1},{1,0},{2,3},{3,2},{4,5},{5,4},{6,7},{7,6},{8,9},{9,8},{10,11... | collective-permute-start | bytes 786440 | tf_op jit(solution)/shard_map/ppermute | solution.py:367
  (130 other events, 1226.5 us)
Sparse Core Ops, SparseCore 0:
  456.9 151.6 all-reduce.5

commit v2 on v0

--- a/solution.py
+++ b/solution.py
@@ -1,6 +1,10 @@
+import functools
+
 import jax
 import jax.numpy as jnp
 from jax import lax
+from jax.experimental import pallas as pl
+from jax.experimental.pallas import tpu as pltpu
 from jax.sharding import PartitionSpec as P
 
 H = 16
@@ -36,7 +40,7 @@
 
 
 def head_split(matrix):
-    return matrix.reshape(matrix.shape[0], H, HD)
+    return matrix.reshape(matrix.shape[0], -1, HD)
 
 
 def masked_scores(queries, keys, mask):
@@ -85,7 +89,7 @@
     return jnp.dot(left, right, preferred_element_type=jnp.float32)
 
 
-def local(
+def local_rows(
     tokens,
     memory,
     source_len,
@@ -345,6 +349,715 @@
     )
 
 
+LOW = jnp.bfloat16
+F32 = jnp.float32
+SCALE = 0.125
+VMEM = pl.BlockSpec(memory_space=pltpu.VMEM)
+SMEM = pl.BlockSpec(memory_space=pltpu.SMEM)
+ANY = pl.BlockSpec(memory_space=pl.ANY)
+
+
+def shape_of(shape, dtype=LOW):
+    return jax.ShapeDtypeStruct(shape, dtype)
+
+
+def nn(left, right):
+    return jnp.dot(left, right, preferred_element_type=F32)
+
+
+def nt(left, right):
+    return lax.dot_general(left, right, (((1,), (1,)), ((), ())), preferred_element_type=F32)
+
+
+def tn(left, right):
+    return lax.dot_general(left, right, (((0,), (0,)), ((), ())), preferred_element_type=F32)
+
+
+def cols(start, size):
+    return pl.ds(pl.multiple_of(start, 128), size)
+
+
+def ln(value, gain, shift):
+    centre = value - jnp.mean(value, axis=-1, keepdims=True)
+    inv = lax.rsqrt(jnp.mean(centre * centre, axis=-1, keepdims=True) + EPSILON)
+    unit = centre * inv
+    return unit * gain + shift, unit, inv
+
+
+def ln_back(grad, unit, inv, gain):
+    scaled = grad * gain
+    return inv * (
+        scaled
+        - jnp.mean(scaled, axis=-1, keepdims=True)
+        - unit * jnp.mean(scaled * unit, axis=-1, keepdims=True)
+    )
+
+
+def gelu_both(value):
+    cdf = 0.5 * (1.0 + lax.erf(value * 0.7071067811865476))
+    return value * cdf, cdf + value * (jnp.exp(-0.5 * value * value) * 0.3989422804014327)
+
+
+def stacked(block):
+    first = lax.broadcasted_iota(jnp.int32, block.shape, 1) < 64
+    zero = jnp.zeros_like(block)
+    return jnp.concatenate([jnp.where(first, block, zero), jnp.where(first, zero, block)], 0)
+
+
+def unstacked(both, n):
+    return jnp.concatenate([both[:64, :n], both[64:, n:]], 0).T
+
+
+def pre_mask(shape, count):
+    return lax.broadcasted_iota(jnp.int32, shape, 0) < count
+
+
+def soft_pair(qs, k_pre, k_blocks, vt_pre, vt_blocks, biases, count):
+    s_pre = nt(k_pre, qs)
+    s_pre = jnp.where(pre_mask(s_pre.shape, count), s_pre, MASKED)
+    s_blocks = [nt(k, qs) + b for k, b in zip(k_blocks, biases)]
+    top = jnp.max(s_pre, axis=0, keepdims=True)
+    for s in s_blocks:
+        top = jnp.maximum(top, jnp.max(s, axis=0, keepdims=True))
+    e_pre = jnp.exp(s_pre - top)
+    total = jnp.sum(e_pre, axis=0, keepdims=True)
+    out = nn(vt_pre, e_pre.astype(LOW))
+    for s, vt in zip(s_blocks, vt_blocks):
+        e = jnp.exp(s - top)
+        total += jnp.sum(e, axis=0, keepdims=True)
+        out += nn(vt, e.astype(LOW))
+    return out * (1.0 / total), top + jnp.log(total)
+
+
+def soft_pair_back(qs, dos, lse, k_pre, v_pre, kt_pre, ks, vs, kts, biases, count):
+    s_pre = nt(k_pre, qs)
+    p_pre = jnp.where(pre_mask(s_pre.shape, count), jnp.exp(s_pre - lse), 0.0)
+    d_pre = nt(v_pre, dos)
+    delta = jnp.sum(p_pre * d_pre, axis=0, keepdims=True)
+    ps, ds = [], []
+    for k, v, b in zip(ks, vs, biases):
+        p = jnp.exp(nt(k, qs) + b - lse)
+        d = nt(v, dos)
+        delta += jnp.sum(p * d, axis=0, keepdims=True)
+        ps.append(p)
+        ds.append(d)
+    g_pre = (p_pre * (d_pre - delta)).astype(LOW)
+    dq = nn(kt_pre, g_pre)
+    dk, dv = [nn(g_pre, qs)], [nn(p_pre.astype(LOW), dos)]
+    for p, d, kt in zip(ps, ds, kts):
+        g = (p * (d - delta)).astype(LOW)
+        dq += nn(kt, g)
+        dk.append(nn(g, qs))
+        dv.append(nn(p.astype(LOW), dos))
+    return dq, dk, dv
+
+
+def self_bias(kpos_ref, qpos_ref, t):
+    seen = kpos_ref[...] <= qpos_ref[:, t * 128 : (t + 1) * 128]
+    bias = jnp.where(seen, 0.0, MASKED)
+    return jnp.concatenate([bias, bias], 1)
+
+
+def self_fwd_kernel(
+    count, ids, tok_a, tok_b, w0, w1, w2, w3, pre, pre_t, kpos, qpos, q_ref, k_ref, v_ref, o_ref, lse_ref, vt
+):
+    for t, tok in enumerate((tok_a, tok_b)):
+        rows = slice(t * 256, (t + 1) * 256)
+        for j, out in enumerate((q_ref, k_ref, v_ref)):
+            acc = None
+            for n, w in enumerate((w0, w1, w2, w3)):
+                term = nn(tok[:, cols(ids[n] * 256, 256)], w[j])
+                acc = term if acc is None else acc + term
+            out[rows, :] = (acc * SCALE if j == 0 else acc).astype(LOW)
+    vt[...] = v_ref[...].T
+    for t in range(4):
+        bias = self_bias(kpos, qpos, t)
+        for p in range(2):
+            lanes = slice(p * 128, (p + 1) * 128)
+            qs = stacked(q_ref[t * 128 : (t + 1) * 128, lanes])
+            out, lse = soft_pair(
+                qs, pre[0, :, lanes], [k_ref[:, lanes]], pre_t[1, lanes, :], [vt[lanes, :]], [bias], count
+            )
+            o_ref[t, :, lanes] = unstacked(out, 128).astype(LOW)
+            lse_ref[p, t] = lse
+
+
+def self_fwd(ids, tok_a, tok_b, ws, pre, pre_t, kpos, qpos, count):
+    return pl.pallas_call(
+        functools.partial(self_fwd_kernel, count),
+        in_specs=[SMEM] + [VMEM] * 10,
+        out_specs=[VMEM] * 5,
+        out_shape=[
+            shape_of((512, 256)),
+            shape_of((512, 256)),
+            shape_of((512, 256)),
+            shape_of((4, 128, 256)),
+            shape_of((2, 4, 1, 256), F32),
+        ],
+        scratch_shapes=[pltpu.VMEM((256, 512), LOW)],
+        compiler_params=pltpu.CompilerParams(vmem_limit_bytes=40 * 2**20),
+        name="self_fwd",
+    )(ids, tok_a, tok_b, *ws, pre, pre_t, kpos, qpos)
+
+
+def self_bwd_kernel(
+    count, ids, q, k, v, do_ref, lse_ref, w0, w1, w2, w3, pre, pre_t, kpos, qpos, part_ref, gpre_ref, kt, dq, dk, dv
+):
+    kt[...] = k[...].T
+    for t in range(4):
+        bias = self_bias(kpos, qpos, t)
+        for p in range(2):
+            lanes = slice(p * 128, (p + 1) * 128)
+            qs = stacked(q[t * 128 : (t + 1) * 128, lanes])
+            dos = stacked(do_ref[t, :, lanes])
+            g, gk, gv = soft_pair_back(
+                qs,
+                dos,
+                lse_ref[p, t],
+                pre[0, :, lanes],
+                pre[1, :, lanes],
+                pre_t[0, lanes, :],
+                [k[:, lanes]],
+                [v[:, lanes]],
+                [kt[lanes, :]],
+                [bias],
+                count,
+            )
+            dq[t * 128 : (t + 1) * 128, lanes] = unstacked(g, 128).astype(LOW)
+            if t == 0:
+                gpre_ref[0, :, lanes] = gk[0]
+                gpre_ref[1, :, lanes] = gv[0]
+                dk[:, lanes] = gk[1]
+                dv[:, lanes] = gv[1]
+            else:
+                gpre_ref[0, :, lanes] += gk[0]
+                gpre_ref[1, :, lanes] += gv[0]
+                dk[:, lanes] += gk[1]
+                dv[:, lanes] += gv[1]
+    dkl, dvl = dk[...].astype(LOW), dv[...].astype(LOW)
+    for n, w in enumerate((w0, w1, w2, w3)):
+        part_ref[:, cols(ids[n] * 256, 256)] = (
+            nt(dq[...], w[0]) * SCALE + nt(dkl, w[1]) + nt(dvl, w[2])
+        ).astype(LOW)
+
+
+def self_bwd(ids, q, k, v, do, lse, ws, pre, pre_t, kpos, qpos, count):
+    return pl.pallas_call(
+        functools.partial(self_bwd_kernel, count),
+        in_specs=[SMEM] + [VMEM] * 13,
+        out_specs=[VMEM] * 2,
+        out_shape=[shape_of((512, 1024)), shape_of((2, 32, 256), F32)],
+        scratch_shapes=[
+            pltpu.VMEM((256, 512), LOW),
+            pltpu.VMEM((512, 256), LOW),
+            pltpu.VMEM((512, 256), F32),
+            pltpu.VMEM((512, 256), F32),
+        ],
+        compiler_params=pltpu.CompilerParams(vmem_limit_bytes=40 * 2**20),
+        name="self_bwd",
+    )(ids, q, k, v, do, lse, *ws, pre, pre_t, kpos, qpos)
+
+
+def part_sizes(parts):
+    return [p.shape[1] for p in parts]
+
+
+def mm(x_ref, parts, ids, j):
+    acc = None
+    for n, part in enumerate(parts):
+        size = part.shape[1]
+        term = nn(x_ref[:, cols(ids[4 + n] * 128, size)], part[j])
+        acc = term if acc is None else acc + term
+    return acc
+
+
+def mem_kernel(ids, mem, *refs):
+    parts, out = refs[:6], refs[6]
+    for j in range(2):
+        out[j] = mm(mem, parts, ids, j).astype(LOW)
+
+
+def mem_fwd(ids, mem, parts):
+    return pl.pallas_call(
+        mem_kernel,
+        in_specs=[SMEM] + [VMEM] * 7,
+        out_specs=VMEM,
+        out_shape=shape_of((2, 256, 1024)),
+        compiler_params=pltpu.CompilerParams(vmem_limit_bytes=40 * 2**20),
+        name="mem_fwd",
+    )(ids, mem, *parts)
+
+
+def mem_back_kernel(ids, near, far_c, far_y, *refs):
+    parts, out = refs[:6], refs[6]
+    total = [
+        (near[j, :256].astype(F32) + far_c[j, :256].astype(F32) + far_y[j].astype(F32)).astype(LOW)
+        for j in range(2)
+    ]
+    for n, part in enumerate(parts):
+        out[:, cols(ids[4 + n] * 128, part.shape[1])] = (nt(total[0], part[0]) + nt(total[1], part[1])).astype(LOW)
+
+
+def mem_back(ids, near, far_c, far_y, parts):
+    return pl.pallas_call(
+        mem_back_kernel,
+        in_specs=[SMEM] + [VMEM] * 9,
+        out_specs=VMEM,
+        out_shape=shape_of((256, 1024)),
+        compiler_params=pltpu.CompilerParams(vmem_limit_bytes=40 * 2**20),
+        name="mem_back",
+    )(ids, near, far_c, far_y, *parts)
+
+
+def fill_bias(bias, ids):
+    live, c, y = ids[10], ids[11], ids[12]
+    for n in range(8):
+        core = c if n < 4 else 1 - c
+        line = y if n % 4 < 2 else 1 - y
+        first = (2 * (2 * core + n % 2) + line) * 128
+        slot = lax.broadcasted_iota(jnp.int32, (128, 256), 0) + first
+        bias[n * 128 : (n + 1) * 128, :] = jnp.where(slot < live, 0.0, MASKED)
+
+
+def mid_fwd_kernel(
+    count, ids, o0, o1, o2, o3, tok, gain, shift, pre, pre_t, mkv_a, mkv_b, *refs
+):
+    parts, outs, (bias, flat) = refs[:6], refs[6:14], refs[14:]
+    cq_ref, lse_ref, unit1, inv1, h2_ref, unit2, inv2, h2l = outs
+    for n, o in enumerate((o0, o1, o2, o3)):
+        flat[:, cols(ids[13 + n] * 256, 256)] = o[...]
+    fill_bias(bias, ids)
+    h1, unit, inv = ln(tok[...].astype(F32) + mm(flat, parts, ids, 0), gain[0:1], shift[0:1])
+    unit1[...] = unit
+    inv1[...] = inv
+    flat[...] = h1.astype(LOW)
+    cq_ref[...] = (mm(flat, parts, ids, 1) * SCALE).astype(LOW)
+    for p in range(8):
+        lanes = slice(p * 128, (p + 1) * 128)
+        qs = stacked(cq_ref[:, lanes])
+        out, lse = soft_pair(
+            qs,
+            pre[0, :, lanes],
+            [mkv_a[0, :, lanes], mkv_b[0, :, lanes]],
+            pre_t[1, lanes, :],
+            [mkv_a[1, :, lanes].T, mkv_b[1, :, lanes].T],
+            [bias[:512], bias[512:]],
+            count,
+        )
+        flat[:, lanes] = unstacked(out, 128).astype(LOW)
+        lse_ref[p] = lse
+    h2, unit, inv = ln(h1 + mm(flat, parts, ids, 2), gain[1:2], shift[1:2])
+    h2_ref[...] = h2
+    unit2[...] = unit
+    inv2[...] = inv
+    h2l[...] = h2.astype(LOW)
+
+
+def mid_fwd(ids, os, tok, gain, shift, pre, pre_t, mkv_a, mkv_b, parts, count):
+    wide = shape_of((128, 1024), F32)
+    thin = shape_of((128, 1), F32)
+    return pl.pallas_call(
+        functools.partial(mid_fwd_kernel, count),
+        in_specs=[SMEM] + [VMEM] * 17,
+        out_specs=[VMEM] * 8,
+        out_shape=[shape_of((128, 1024)), shape_of((8, 1, 256), F32), wide, thin, wide, wide, thin, shape_of((128, 1024))],
+        scratch_shapes=[pltpu.VMEM((1024, 256), F32), pltpu.VMEM((128, 1024), LOW)],
+        compiler_params=pltpu.CompilerParams(vmem_limit_bytes=48 * 2**20),
+        name="mid_fwd",
+    )(ids, *os, tok, gain, shift, pre, pre_t, mkv_a, mkv_b, *parts)
+
+
+def mlp_kernel(ids, h2, h2l, unit2, inv2, cot, gain, shift, down_b, up_b, down_any, up_any, *refs):
+    parts, outs, scratch = refs[:6], refs[6:12], refs[12:]
+    mixed, dr2, gau, gadt, gaub, gadb = outs
+    bufs, (down, up, act, slope, acc, sems) = scratch[:6], scratch[6:]
+    copies = []
+    for n in range(6):
+        copies.append([pltpu.make_async_copy(parts[n].at[pl.ds(4 * h, 4)], bufs[n].at[pl.ds(4 * h, 4)], sems.at[2 * n + h]) for h in range(2)])
+    ad = [pltpu.make_async_copy(down_any, down, sems.at[12]), pltpu.make_async_copy(up_any, up, sems.at[13])]
+    for n in range(6):
+        copies[n][0].start()
+    ad[0].start()
+    ad[1].start()
+    for n in range(6):
+        copies[n][1].start()
+    for n in range(6):
+        copies[n][0].wait()
+    for s in range(4):
+        u = mm(h2l, bufs, ids, s)
+        lanes = slice(s * 1024, (s + 1) * 1024)
+        value, gradient = gelu_both(u)
+        act[:, lanes] = value.astype(LOW)
+        slope[:, lanes] = gradient
+    ad[0].wait()
+    ad[1].wait()
+    down_w, up_w = down[...].astype(LOW), up[...].astype(LOW)
+    a, a_slope = gelu_both(nn(h2l[...], down_w) + down_b[...])
+    a = a.astype(LOW)
+    adapted = nn(a, up_w) + up_b[...]
+    total = h2[...] + 4.0 * adapted
+    for n in range(6):
+        copies[n][1].wait()
+
+    def rows(n, s):
+        return (ids[4 + n] // 2) * 1024 + s * 256 + (ids[4 + n] % 2) * 128
+
+    for s in range(4):
+        for n, buf in enumerate(bufs):
+            total += nn(act[:, cols(rows(n, s), buf.shape[1])], buf[4 + s])
+    out, unit3, inv3 = ln(total, gain[2:3], shift[2:3])
+    mixed[...] = out.astype(LOW)
+    dr3 = ln_back(cot[...].astype(F32), unit3, inv3, gain[2:3])
+    dffn = dr3.astype(LOW)
+    dad = (4.0 * dr3).astype(LOW)
+    gau[...] = tn(a, dad)
+    gaub[...] = jnp.sum(dad.astype(F32), axis=0, keepdims=True)
+    ddn = (a_slope * nt(dad, up_w)).astype(LOW)
+    gadt[...] = tn(ddn, h2l[...])
+    gadb[...] = jnp.sum(ddn.astype(F32), axis=0, keepdims=True)
+    for s in range(4):
+        for n, buf in enumerate(bufs):
+            where = cols(rows(n, s), buf.shape[1])
+            act[:, where] = (slope[:, where] * nt(dffn, buf[4 + s])).astype(LOW)
+    for n, buf in enumerate(bufs):
+        term = nt(act[:, :1024], buf[0])
+        for s in range(1, 4):
+            term += nt(act[:, s * 1024 : (s + 1) * 1024], buf[s])
+        acc[:, cols(ids[4 + n] * 128, buf.shape[1])] = term
+    dh2 = dr3 + acc[...] + nt(ddn, down_w)
+    dr2[...] = ln_back(dh2, unit2[...], inv2[...], gain[1:2])
+
+
+def mlp(ids, h2, h2l, unit2, inv2, cot, gain, shift, down_b, up_b, down, up, parts):
+    return pl.pallas_call(
+        mlp_kernel,
+        in_specs=[SMEM] + [VMEM] * 9 + [ANY] * 8,
+        out_specs=[VMEM] * 6,
+        out_shape=[
+            shape_of((128, 1024)),
+            shape_of((128, 1024), F32),
+            shape_of((512, 1024), F32),
+            shape_of((512, 1024), F32),
+            shape_of((1, 1024), F32),
+            shape_of((1, 512), F32),
+        ],
+        scratch_shapes=[pltpu.VMEM(p.shape, LOW) for p in parts]
+        + [
+            pltpu.VMEM((1024, 512), F32),
+            pltpu.VMEM((512, 1024), F32),
+            pltpu.VMEM((128, 4096), LOW),
+            pltpu.VMEM((128, 4096), F32),
+            pltpu.VMEM((128, 1024), F32),
+            pltpu.SemaphoreType.DMA((14,)),
+        ],
+        compiler_params=pltpu.CompilerParams(vmem_limit_bytes=56 * 2**20),
+        name="mlp",
+    )(ids, h2, h2l, unit2, inv2, cot, gain, shift, down_b, up_b, down, up, *parts)
+
+
+def mid_bwd_kernel(count, ids, dr2, cq, lse, unit1, inv1, gain, pre, pre_t, mkv_a, mkv_b, *refs):
+    parts, outs, (bias, flat, wide) = refs[:6], refs[6:11], refs[11:]
+    near, far, gpre, dr1, do_ref = outs
+    fill_bias(bias, ids)
+
+    def back(value, j):
+        for n, part in enumerate(parts):
+            wide[:, cols(ids[4 + n] * 128, part.shape[1])] = nt(value, part[j])
+
+    back(dr2[...].astype(LOW), 2)
+    flat[...] = wide[...].astype(LOW)
+    for p in range(8):
+        lanes = slice(p * 128, (p + 1) * 128)
+        qs = stacked(cq[:, lanes])
+        dos = stacked(flat[:, lanes])
+        g, gk, gv = soft_pair_back(
+            qs,
+            dos,
+            lse[p],
+            pre[0, :, lanes],
+            pre[1, :, lanes],
+            pre_t[0, lanes, :],
+            [mkv_a[0, :, lanes], mkv_b[0, :, lanes]],
+            [mkv_a[1, :, lanes], mkv_b[1, :, lanes]],
+            [mkv_a[0, :, lanes].T, mkv_b[0, :, lanes].T],
+            [bias[:512], bias[512:]],
+            count,
+        )
+        for j, got in enumerate((gk, gv)):
+            gpre[j, :, lanes] = got[0]
+            near[j, :, lanes] = got[1].astype(LOW)
+            far[j, :, lanes] = got[2].astype(LOW)
+        flat[:, lanes] = unstacked(g, 128).astype(LOW)
+    back(flat[...], 1)
+    dh1 = dr2[...] + SCALE * wide[...]
+    grad = ln_back(dh1, unit1[...], inv1[...], gain[0:1])
+    dr1[...] = grad
+    back(grad.astype(LOW), 0)
+    for n in range(4):
+        do_ref[n] = wide[:, cols(ids[13 + n] * 256, 256)].astype(LOW)
+
+
+def mid_bwd(ids, dr2, cq, lse, unit1, inv1, gain, pre, pre_t, mkv_a, mkv_b, parts, count):
+    return pl.pallas_call(
+        functools.partial(mid_bwd_kernel, count),
+        in_specs=[SMEM] + [VMEM] * 16,
+        out_specs=[VMEM] * 5,
+        out_shape=[
+            shape_of((2, 512, 1024)),
+            shape_of((2, 512, 1024)),
+            shape_of((2, 32, 1024), F32),
+            shape_of((128, 1024), F32),
+            shape_of((4, 128, 256)),
+        ],
+        scratch_shapes=[
+            pltpu.VMEM((1024, 256), F32),
+            pltpu.VMEM((128, 1024), LOW),
+            pltpu.VMEM((128, 1024), F32),
+        ],
+        compiler_params=pltpu.CompilerParams(vmem_limit_bytes=52 * 2**20),
+        name="mid_bwd",
+    )(ids, dr2, cq, lse, unit1, inv1, gain, pre, pre_t, mkv_a, mkv_b, *parts)
+
+
+def pack_kernel(sources, ids, *refs):
+    n_args = max(a for a, *_ in sources) + 1
+    args, (own, half), (wide, low_buf, in_sem, own_sem, half_sem) = refs[:n_args], refs[n_args : n_args + 2], refs[n_args + 2 :]
+    y = ids[12]
+    count = len(sources)
+
+    def fetch(m):
+        a, lead, row, col = sources[m]
+        src = args[a] if lead is None else args[a].at[lead]
+        return pltpu.make_async_copy(src.at[pl.ds(row, 256), pl.ds(col, 1024)], wide.at[m % 3], in_sem.at[m % 3])
+
+    def store(m):
+        return (
+            pltpu.make_async_copy(low_buf.at[m % 3], own.at[m], own_sem.at[m % 3]),
+            pltpu.make_async_copy(low_buf.at[m % 3, pl.ds(pl.multiple_of(y * 128, 128), 128)], half.at[m], half_sem.at[m % 3]),
+        )
+
+    for m in range(min(2, count)):
+        fetch(m).start()
+    for m in range(count):
+        if m + 2 < count:
+            fetch(m + 2).start()
+        fetch(m).wait()
+        if m >= 3:
+            for s in store(m - 3):
+                s.wait()
+        low_buf[m % 3] = wide[m % 3].astype(LOW)
+        for s in store(m):
+            s.start()
+    for m in range(max(0, count - 3), count):
+        for s in store(m):
+            s.wait()
+
+
+def pack(ids, sources, *args):
+    count = len(sources)
+    return pl.pallas_call(
+        functools.partial(pack_kernel, sources),
+        in_specs=[SMEM] + [ANY] * len(args),
+        out_specs=[ANY] * 2,
+        out_shape=[shape_of((count, 256, 1024)), shape_of((count, 128, 1024))],
+        scratch_shapes=[
+            pltpu.VMEM((3, 256, 1024), F32),
+            pltpu.VMEM((3, 256, 1024), LOW),
+            pltpu.SemaphoreType.DMA((3,)),
+            pltpu.SemaphoreType.DMA((3,)),
+            pltpu.SemaphoreType.DMA((3,)),
+        ],
+        compiler_params=pltpu.CompilerParams(vmem_limit_bytes=16 * 2**20),
+        name="pack",
+    )(ids, *args)
+
+
+AXES = ("row", "seq")
+
+
+def pairs_of(target):
+    pairs = []
+    for source in range(32):
+        row, seq = divmod(source, 8)
+        x, c, z, y = target(*divmod(row, 2), *divmod(seq, 2))
+        pairs.append((source, (2 * x + c) * 8 + 2 * z + y))
+    return pairs
+
+
+SWAP_X = pairs_of(lambda x, c, z, y: (1 - x, c, z, y))
+SWAP_C = pairs_of(lambda x, c, z, y: (x, 1 - c, z, y))
+SWAP_Y = pairs_of(lambda x, c, z, y: (x, c, z, 1 - y))
+TURN = [pairs_of(lambda x, c, z, y, r=r: (x, z // 2, 2 * c + (z + r) % 2, y)) for r in range(2)]
+
+
+def send(value, pairs):
+    return lax.ppermute(value, AXES, pairs)
+
+
+def turn(first, second, odd):
+    out = [send(jnp.where(odd, second, first), TURN[0]), send(jnp.where(odd, first, second), TURN[1])]
+    return jnp.where(odd, out[1], out[0]), jnp.where(odd, out[0], out[1])
+
+
+def local_pairs(
+    tokens,
+    memory,
+    source_len,
+    bucket_order,
+    prefix_self,
+    prefix_cross,
+    self_query,
+    self_kv,
+    self_out,
+    cross_query,
+    cross_kv,
+    cross_out,
+    fc_in,
+    fc_out,
+    ln_gain,
+    ln_bias,
+    ad_down,
+    ad_down_bias,
+    ad_up,
+    ad_up_bias,
+    cotangent,
+):
+    low = jnp.bfloat16
+    f32 = jnp.float32
+    row, seq = lax.axis_index("row"), lax.axis_index("seq")
+    x, c, z, y = row // 2, row % 2, seq // 2, seq % 2
+    odd = z % 2 == 1
+    count = prefix_self.shape[1]
+
+    live = send(jnp.where(odd, source_len[1], source_len[0]).reshape(1, 1), TURN[0])[0, 0]
+    group = 2 * y + c
+    far_row = 2 * (row ^ 2)
+    both_row = 2 * (row ^ 3)
+    ids = jnp.stack(
+        [row, row ^ 1, row ^ 2, row ^ 3]
+        + [2 * row, 2 * (row ^ 1), far_row + y, far_row + 1 - y, both_row + y, both_row + 1 - y]
+        + [jnp.int32(0), c, y]
+        + [group, group ^ 2, group ^ 1, group ^ 3]
+    ).astype(jnp.int32)
+    ids_live = ids.at[10].set(live)
+
+    tok_own = jnp.concatenate(turn(tokens[0], tokens[1], odd), 0)
+    mem_own = jnp.concatenate(turn(memory[0], memory[1], odd), 0)
+    cot_own = jnp.concatenate(turn(cotangent[0], cotangent[1], odd), 0)
+    tok_a = jnp.concatenate([tok_own, send(tok_own, SWAP_Y)], 0)
+    tok_b = send(tok_a, SWAP_C)
+
+    places = (bucket_order[:, None] * 32 + jnp.arange(32, dtype=jnp.int32)[None]).reshape(2, 2, 2, 64)
+    places = places.transpose(0, 2, 1, 3)
+    places = jnp.where(c == 0, places, places[::-1])
+    places = jnp.where(y == 0, places, places[:, ::-1])
+    kpos, qpos = places.reshape(512, 1), places.reshape(1, 512)
+
+    packed = jnp.stack([self_query, self_kv[0], self_kv[1]])
+    packed = lax.dynamic_slice_in_dim(packed.reshape(3, 256, 2, 512), y, 1, 2).reshape(3, 256, 2, 256)
+    packed = packed.astype(low).transpose(2, 0, 1, 3)
+    far = send(packed, SWAP_X)
+    keep, give = jnp.where(c == 0, packed[0], packed[1]), jnp.where(c == 0, packed[1], packed[0])
+    far_keep, far_give = jnp.where(c == 0, far[0], far[1]), jnp.where(c == 0, far[1], far[0])
+    head_parts = [keep, send(give, SWAP_C), far_keep, send(far_give, SWAP_C)]
+
+    def whole(sources, *arrays):
+        own, half = pack(ids, sources, *arrays)
+        near = send(half, SWAP_X)
+        return (own, send(own, SWAP_C)), near
+
+    def rest(own, near):
+        other = send(near, SWAP_Y)
+        return (*own, near, other, send(near, SWAP_C), send(other, SWAP_C))
+
+    ckv_parts = rest(*whole([(0, 0, 0, 0), (0, 1, 0, 0)], cross_kv))
+    mid_parts = rest(
+        *whole([(n, None, 0, 0) for n in range(3)], self_out, cross_query, cross_out)
+    )
+    ffn_parts = rest(
+        *whole(
+            [(0, None, 0, s * 1024) for s in range(4)] + [(1, None, s * 256, 0) for s in range(4)],
+            fc_in,
+            fc_out,
+        )
+    )
+
+    def padded(prefix):
+        wide = jnp.pad(prefix.astype(low), ((0, 0), (0, 32 - count), (0, 0)))
+        return wide, wide.transpose(0, 2, 1)
+
+    pre_c, pre_ct = padded(prefix_cross)
+    pre_s, pre_st = padded(lax.dynamic_slice_in_dim(prefix_self, group * 256, 256, 2))
+
+    mkv = mem_fwd(ids, mem_own, ckv_parts)
+    mkv_a = jnp.concatenate([mkv, send(mkv, SWAP_Y)], 1)
+    mkv_b = send(mkv_a, SWAP_C)
+
+    q, k, v, att, self_lse = self_fwd(ids, tok_a, tok_b, head_parts, pre_s, pre_st, kpos, qpos, count)
+    got = send(jnp.stack([att[1], att[3]]), SWAP_Y)
+    got_c = send(jnp.stack([att[2], got[1]]), SWAP_C)
+
+    cq, cross_lse, unit1, inv1, h2, unit2, inv2, h2l = mid_fwd(
+        ids_live,
+        (att[0], got[0], got_c[0], got_c[1]),
+        tok_own,
+        ln_gain,
+        ln_bias,
+        pre_c,
+        pre_ct,
+        mkv_a,
+        mkv_b,
+        mid_parts,
+        count,
+    )
+    mixed, dr2, gau, gadt, gaub, gadb = mlp(
+        ids,
+        h2,
+        h2l,
+        unit2,
+        inv2,
+        cot_own,
+        ln_gain,
+        ln_bias,
+        ad_down_bias[None],
+        ad_up_bias[None],
+        ad_down,
+        ad_up,
+        ffn_parts,
+    )
+    mixed = mixed.reshape(2, 64, 1024)
+    mixed = jnp.stack(turn(mixed[0], mixed[1], odd))
+
+    near, far_c, gpre_cross, dr1, grad_att = mid_bwd(
+        ids_live, dr2, cq, cross_lse, unit1, inv1, ln_gain, pre_c, pre_ct, mkv_a, mkv_b, mid_parts, count
+    )
+
+    got_c = send(grad_att[2:], SWAP_C)
+    got = send(jnp.stack([grad_att[1], got_c[1]]), SWAP_Y)
+    grad_o = jnp.stack([grad_att[0], got[0], got_c[0], got[1]])
+    part, gpre_self = self_bwd(
+        ids, q, k, v, grad_o, self_lse, head_parts, pre_s, pre_st, kpos, qpos, count
+    )
+
+    got_c = send(far_c, SWAP_C)
+    got = send((near[:, 256:].astype(f32) + got_c[:, 256:].astype(f32)).astype(low), SWAP_Y)
+    d_memory = mem_back(ids, near, got_c, got, ckv_parts).reshape(2, 128, 1024)
+    d_memory = jnp.stack(turn(d_memory[0], d_memory[1], odd))
+
+    half = part[:256].astype(f32) + send(part[256:], SWAP_C).astype(f32)
+    d_tokens = dr1 + half[:128] + send(half[128:].astype(low), SWAP_Y).astype(f32)
+    d_tokens = d_tokens.astype(low).reshape(2, 64, 1024)
+    d_tokens = jnp.stack(turn(d_tokens[0], d_tokens[1], odd))
+
+    pre_self_grad = lax.dynamic_update_slice_in_dim(
+        jnp.zeros(prefix_self.shape, f32), gpre_self[:, :count], group * 256, 2
+    )
+    totals = lax.psum(
+        (pre_self_grad, gpre_cross[:, :count], gadt, gadb[0], gau, gaub[0]), ("row", "seq")
+    )
+    return (mixed, d_tokens, d_memory, totals[0], totals[1], totals[2].T, *totals[3:])
+
+
 def solution(mesh):
     in_specs = (
         P("row", "seq", None),
@@ -380,4 +1093,5 @@
         P(),
         P(),
     )
+    local = local_pairs if (mesh.shape["row"], mesh.shape["seq"]) == (4, 8) else local_rows
     return jax.shard_map(local, mesh=mesh, in_specs=in_specs, out_specs=out_specs, check_vma=False)

time: 1330 us -> 453 us (0.34)
  waiting for transfers between devices: 984 us -> 196 us
  matrix products: 126 us -> 0 us
  local copies, waits for them, and re-layouts: 123 us -> 45.4 us
  Pallas kernels: 0 us -> 70.9 us
  starting transfers between devices: 1.34 us -> 53.3 us
  other arithmetic: 38.3 us -> 19.7 us
    all_gather x12 -> x0, waiting for transfers between devices: 424 us -> none  [the longest x1 70.6 us: local(): lax.all_gather(mem_keys, 'seq', axis=1, tiled=True)]
    reduce_scatter x8 -> x0, waiting for transfers between devices: 414 us -> none  [the longest x2 140 us: local(): lax.psum_scatter(cross_grads[row_index][1][prefix_count:].astype(jnp.bflo...]
    ppermute x0 -> x43, waiting for transfers between devices: none -> 137 us  [send(): return lax.ppermute(value, AXES, pairs)]
    dot_general x49 -> x0, matrix products: 126 us -> none  [the longest x23 75.6 us: project(): return jnp.dot(left, right, preferred_element_type=jnp.float32)]
    psum x1, waiting for transfers between devices: 146 us -> 59.6 us  [local_pairs(): lax.psum((pre_self_grad, gpre_cross[:, :count], gadt, gadb[0], gau, gaub[...]
    pallas_call x0 -> x10, Pallas kernels: none -> 70.9 us  [the longest x1 19.5 us: mlp(): pl.pallas_call(mlp_kernel, in_specs=[SMEM] + [VMEM] * 9 + [ANY] * 8, out_...]
    ppermute x0 -> x43, starting transfers between devices: none -> 53.3 us  [send(): return lax.ppermute(value, AXES, pairs)]
    slice x33 -> x9, local copies, waits for them, and re-layouts: 51.2 us -> 3.87 us  [the longest x1 1.94 us: local_pairs(): half = part[:256].astype(f32) + send(part[256:], SWAP_C).astype(f32)]
  transfers between devices with their start and end apart: 21 -> 44, of which waited for: 19 -> 12; matrix products, arithmetic and copies ran while one was open for 14% -> 9% of each run, Pallas kernels for 0% -> 8%
where the time goes in v2:
time: 453 us; the launch traced here: 445 us
  waiting for transfers between devices  196 us (43%)
  Pallas kernels  70.9 us (16%)
  starting transfers between devices  53.3 us (12%)
  local copies, waits for them, and re-layouts  45.4 us (10%)
  blocking collectives  43.2 us (10%)
  other arithmetic  19.7 us (4%)
  between operations  16.7 us (4%)
    ppermute x43, waiting for transfers between devices, send(): return lax.ppermute(value, AXES, pairs)  137 us
    psum x1, waiting for transfers between devices, local_pairs(): lax.psum((pre_self_grad, gpre_cross[:, :count], gadt, gadb[0], gau, gaub[...  59.6 us
    ppermute x43, starting transfers between devices, send(): return lax.ppermute(value, AXES, pairs)  53.3 us
    psum x1, blocking collectives, local_pairs(): lax.psum((pre_self_grad, gpre_cross[:, :count], gadt, gadb[0], gau, gaub[...  43.2 us
    unnamed x174, local copies, waits for them, and re-layouts  33.7 us
    pallas_call x1, Pallas kernels, mlp(): pl.pallas_call(mlp_kernel, in_specs=[SMEM] + [VMEM] * 9 + [ANY] * 8, out_...  19.5 us
    pallas_call x1, Pallas kernels, mid_bwd(): pl.pallas_call(functools.partial(mid_bwd_kernel, count), in_specs=[SMEM]...  15.2 us
    pallas_call x1, Pallas kernels, mid_fwd(): pl.pallas_call(functools.partial(mid_fwd_kernel, count), in_specs=[SMEM]...  11 us
  transfers between devices with their start and end apart: 44, of which 12 were waited for; matrix products, arithmetic and copies ran while one was open for 9% of the time, Pallas kernels for 8%

profile of v2, /device:TPU:0, one launch (start us, length us, event | category | flops | bytes accessed | tf_op | source)
XLA Modules:
  0.0 445.2 jit_solution(2709459115458365790)
XLA Ops:
  9.2 3.0 collective-permute-start.10
  23.8 3.5 pack.5
  44.9 7.6 %collective-permute-start.5 = (bf16[3,256,256]{2,1,0:T(8,128)(2,1)}, bf16[3,256,256]{2,1,0:T(8,128)(2,1)S(1)}, u32[]{:S(2)}, u32[]{:S(2)}) collective-permute-start(bf16[3,256,256]{2,1,0:T(8,128)(2,1)} %get-tuple-element.129), channel_id=1, source_target_pairs={{0,8},{1,9},{2,10},{3,11},{4,12},{5,13},{6,14},{7,15},{8,0},{9,1},... | collective-permute-start | bytes 1179656 | tf_op jit(solution)/shard_map/ppermute | solution.py:894
  52.5 5.3 %collective-permute-start.4 = (bf16[256,1024]{1,0:T(8,128)(2,1)}, bf16[256,1024]{1,0:T(8,128)(2,1)}, u32[]{:S(2)}, u32[]{:S(2)}) collective-permute-start(bf16[256,1024]{1,0:T(8,128)(2,1)} %pad_maximum_fusion.1.tok_a), channel_id=1, source_target_pairs={{0,8},{1,9},{2,10},{3,11},{4,12},{5,13},{6,14},{7,15},{8,0},{9,1},... | collective-permute-start | bytes 1572872 | tf_op jit(solution)/shard_map/ppermute | solution.py:894
  57.8 34.6 %collective-permute-done.13.refs_2_ = bf16[2,128,1024]{2,1,0:T(8,128)(2,1)} collective-permute-done((bf16[2,128,1024]{2,1,0:T(8,128)(2,1)S(1)}, bf16[2,128,1024]{2,1,0:T(8,128)(2,1)}, u32[]{:S(2)}, u32[]{:S(2)}) %collective-permute-start.13) | collective-permute-done | bytes 524320 | tf_op jit(solution)/shard_map/ppermute | solution.py:894
  105.2 2.4 collective-permute-done.14.refs_3_
  109.6 5.2 %self_fwd.1 = (bf16[512,256]{1,0:T(8,128)(2,1)S(1)}, bf16[512,256]{1,0:T(8,128)(2,1)S(1)}, bf16[512,256]{1,0:T(8,128)(2,1)S(1)}, bf16[4,128,256]{2,1,0:T(8,128)(2,1)S(1)}, f32[2,4,1,256]{3,2,1,0:T(1,128)S(1)}) custom-call(s32[17]{0:T(128)S(1)} %stack.115.ids, bf16[256,1024]{1,0:T(8,128)(2,1)} %pad_maximum_fusion.1.tok_a, ...), custom_call_target="tpu_custom_call" | custom-call | tf_op jit(solution)/shard_map/self_fwd/pallas_call | solution.py:486
  118.4 3.3 mem_fwd.1
  123.4 35.7 %collective-permute-done.8 = bf16[2,128,256]{2,1,0:T(8,128)(2,1)S(1)} collective-permute-done((bf16[2,128,256]{2,1,0:T(8,128)(2,1)S(1)}, bf16[2,128,256]{2,1,0:T(8,128)(2,1)S(1)}, u32[]{:S(2)}, u32[]{:S(2)}) %collective-permute-start.8) | collective-permute-done | bytes 131104 | tf_op jit(solution)/shard_map/ppermute | solution.py:894
  160.6 6.2 %collective-permute-start.9 = (bf16[2,128,256]{2,1,0:T(8,128)(2,1)S(1)}, bf16[2,128,256]{2,1,0:T(8,128)(2,1)S(1)}, u32[]{:S(2)}, u32[]{:S(2)}) collective-permute-start(bf16[2,128,256]{2,1,0:T(8,128)(2,1)S(1)} %pad_maximum_fusion.10), channel_id=1, source_target_pairs={{0,8},{1,9},{2,10},{3,11},{4,12},{5,13},{6,14},{7,15},{8,0},{9,1},... | collective-permute-start | bytes 393224 | tf_op jit(solution)/shard_map/ppermute | solution.py:894
  168.4 13.1 %collective-permute-done.17 = bf16[2,256,1024]{2,1,0:T(8,128)(2,1)S(1)} collective-permute-done((bf16[2,256,1024]{2,1,0:T(8,128)(2,1)S(1)}, bf16[2,256,1024]{2,1,0:T(8,128)(2,1)S(1)}, u32[]{:S(2)}, u32[]{:S(2)}) %collective-permute-start.17) | collective-permute-done | bytes 1048608 | tf_op jit(solution)/shard_map/ppermute | solution.py:894
  183.0 15.1 %collective-permute-done.21.refs_3_ = bf16[3,128,1024]{2,1,0:T(8,128)(2,1)} collective-permute-done((bf16[3,128,1024]{2,1,0:T(8,128)(2,1)S(1)}, bf16[3,128,1024]{2,1,0:T(8,128)(2,1)}, u32[]{:S(2)}, u32[]{:S(2)}) %collective-permute-start.21) | collective-permute-done | bytes 786464 | tf_op jit(solution)/shard_map/ppermute | solution.py:894
  212.8 11.0 %mid_fwd.1 = (bf16[128,1024]{1,0:T(8,128)(2,1)S(1)}, f32[8,1,256]{2,1,0:T(1,128)S(1)}, f32[128,1024]{1,0:T(8,128)S(1)}, f32[128,1]{1,0:T(8,128)S(1)}, f32[128,10...) custom-call(s32[17]{0:T(128)S(1)} %copy-done.58, ...), custom_call_target="tpu_custom_call" | custom-call | tf_op jit(solution)/shard_map/mid_fwd/pallas_call | solution.py:659
  227.7 19.5 %mlp.1 = (bf16[128,1024]{1,0:T(8,128)(2,1)}, f32[128,1024]{1,0:T(8,128)}, f32[512,1024]{1,0:T(8,128)}, f32[512,1024]{1,0:T(8,128)}, f32[1,1024]{1,0:T(1,128)}, /*index=5*/f32[1,512]{1,0:T(1,128)}) custom-call(s32[17]{0:T(128)} %copy-done.52, f32[128,1024]{1,0:T(8,128)} %copy-done.34, bf16[128,1024]{1,0:T(8,128)(2,1)} %copy-done.38, f32[128,1024]{1,0:T(8,128)} %copy-done.35, ...), custom_call_target="tpu_custom_call" | custom-call | tf_op jit(solution)/shard_map/mlp/pallas_call | solution.py:732
  247.2 15.2 %mid_bwd.1 = (bf16[2,512,1024]{2,1,0:T(8,128)(2,1)}, bf16[2,512,1024]{2,1,0:T(8,128)(2,1)}, f32[2,32,1024]{2,1,0:T(8,128)S(1)}, f32[128,1024]{1,0:T(8,128)S(1)}, bf16[4,128,256]{2,1,0:T(8,128)(2,1)S(1)}) custom-call(s32[17]{0:T(128)S(1)} %copy-done.59, f32[128,1024]{1,0:T(8,128)} %get-tuple-element.65.dr2, bf16[128,1024]{1,0:T(8,128)(2,1)S(1)} %get-tuple-element.66.cq, ...), custom_call_target="tpu_custom_call" | custom-call | tf_op jit(solution)/shard_map/mid_bwd/pallas_call | solution.py:801
  263.1 3.7 collective-permute-done.33
  268.5 4.0 collective-permute-done.34
  272.7 6.8 %self_bwd.1 = (bf16[512,1024]{1,0:T(8,128)(2,1)S(1)}, f32[2,32,256]{2,1,0:T(8,128)S(1)}) custom-call(s32[17]{0:T(128)S(1)} %copy-done.53, bf16[512,256]{1,0:T(8,128)(2,1)S(1)} %copy-done.42, bf16[512,256]{1,0:T(8,128)(2,1)S(1)} %copy-done.44, bf16[512,256]{1,0:T(8,128)(2,1)S(1)} %copy-done.46, bf16[4,128,256]{2,1,0:T(8,128)(2,1)S(1)} %pad_maximum_fusion.7.do_ref, ...), custom_call_target="tpu_custom_call" | custom-call | tf_op jit(solution)/shard_map/self_bwd/pallas_call | solution.py:545
  285.9 43.2 %all-reduce.2 = (f32[512]{0:T(512)}, f32[1024]{0:T(1024)}) all-reduce(f32[512]{0:T(512)S(1)} %bitcast.89, f32[1024]{0:T(1024)S(1)} %bitcast.86), channel_id=1, replica_groups=mesh['row'=4,'seq'=8] {'row','seq'}, use_global_device_ids=true, to_apply=%region_3.4 | all-reduce | flops 1536 | bytes 12288 | tf_op jit(solution)/shard_map/psum | solution.py:1055
  330.8 2.6 collective-permute-start.40
  336.6 26.6 %collective-permute-done.36 = bf16[128,1024]{1,0:T(8,128)(2,1)S(1)} collective-permute-done((bf16[128,1024]{1,0:T(8,128)(2,1)S(1)}, bf16[128,1024]{1,0:T(8,128)(2,1)S(1)}, u32[]{:S(2)}, u32[]{:S(2)}) %collective-permute-start.36) | collective-permute-done | bytes 262176 | tf_op jit(solution)/shard_map/ppermute | solution.py:894
  364.3 4.1 mem_back.1
  371.8 59.6 %all-reduce.6.cloned.1.call-done = (f32[2,30,1024]{2,0,1:T(2,128)}, f32[2,30,1024]{2,1,0:T(8,128)}, f32[1024,512]{0,1:T(8,128)}, f32[512,1024]{1,0:T(8,128)}) async-done(((f32[2,30,1024]{2,0,1:T(2,128)}, f32[2,30,1024]{2,1,0:T(8,128)}, f32[1024,512]{0,1:T(8,128)}, f32[512,1024]{1,0:T(8,128)}), (f32[2,30,1024]{2,0,1:T(2,128)}, f32[2,30,1024]{2,1,0:T(8,128)}, f32[1024,512]{0,1:T(8,128)}, ...) | async-done | bytes 4685840 | tf_op jit(solution)/shard_map/psum | solution.py:1055
  431.5 2.9 copy.83
  (314 shorter events, 94.2 us)
Async XLA Ops:
  7.2 424.3 %all-reduce.6.cloned.1.call-start = ((), (), s32[]{:S(2)}) async-start(), calls=%async_computation | async-start | bytes 9404416 | tf_op jit(solution)/shard_map/psum | solution.py:1055
  9.2 35.7 %collective-permute-start.10 = (bf16[128,1024]{1,0:T(8,128)(2,1)}, bf16[128,1024]{1,0:T(8,128)(2,1)S(1)}, u32[]{:S(2)}, u32[]{:S(2)}) collective-permute-start(bf16[128,1024]{1,0:T(8,128)(2,1)} %get-tuple-element.137), channel_id=1, source_target_pairs={{0,2},{1,3},{2,0},{3,1},{4,10},{5,11},{6,8},{7,9},{8,6},{9,7},{10,... | collective-permute-start | bytes 786440 | tf_op jit(solution)/shard_map/ppermute | solution.py:894
  16.6 76.7 %collective-permute-start.6 = (bf16[2,3,256,256]{3,2,1,0:T(8,128)(2,1)}, bf16[2,3,256,256]{3,2,1,0:T(8,128)(2,1)}, u32[]{:S(2)}, u32[]{:S(2)}) collective-permute-start(bf16[2,3,256,256]{3,2,1,0:T(8,128)(2,1)} %bitcast.25), channel_id=1, source_target_pairs={{0,16},{1,17},{2,18},{3,19},{4,20},{5,21},{6,22},{7,23},{8,24},{9,... | collective-permute-start | bytes 2359304 | tf_op jit(solution)/shard_map/ppermute | solution.py:894
  29.4 78.2 %collective-permute-start.27 = (bf16[8,128,1024]{2,1,0:T(8,128)(2,1)}, bf16[8,128,1024]{2,1,0:T(8,128)(2,1)}, u32[]{:S(2)}, u32[]{:S(2)}) collective-permute-start(bf16[8,128,1024]{2,1,0:T(8,128)(2,1)} %get-tuple-element.63), channel_id=1, source_target_pairs={{0,16},{1,17},{2,18},{3,19},{4,20},{5,21},{6,22},{7,23},{8,24},{9,... | collective-permute-start | bytes 6291464 | tf_op jit(solution)/shard_map/ppermute | solution.py:894
  41.2 51.2 %collective-permute-start.13 = (bf16[2,128,1024]{2,1,0:T(8,128)(2,1)S(1)}, bf16[2,128,1024]{2,1,0:T(8,128)(2,1)}, u32[]{:S(2)}, u32[]{:S(2)}) collective-permute-start(bf16[2,128,1024]{2,1,0:T(8,128)(2,1)S(1)} %get-tuple-element.55), channel_id=1, source_target_pairs={{0,16},{1,17},{2,18},{3,19},{4,20},{5,21},{6,22},{7,23},{8,24},{9,... | collective-permute-start | bytes 1572872 | tf_op jit(solution)/shard_map/ppermute | solution.py:894
  44.9 51.9 %collective-permute-start.5 = (bf16[3,256,256]{2,1,0:T(8,128)(2,1)}, bf16[3,256,256]{2,1,0:T(8,128)(2,1)S(1)}, u32[]{:S(2)}, u32[]{:S(2)}) collective-permute-start(bf16[3,256,256]{2,1,0:T(8,128)(2,1)} %get-tuple-element.129), channel_id=1, source_target_pairs={{0,8},{1,9},{2,10},{3,11},{4,12},{5,13},{6,14},{7,15},{8,0},{9,1},... | collective-permute-start | bytes 1179656 | tf_op jit(solution)/shard_map/ppermute | solution.py:894
  52.5 51.2 %collective-permute-start.4 = (bf16[256,1024]{1,0:T(8,128)(2,1)}, bf16[256,1024]{1,0:T(8,128)(2,1)}, u32[]{:S(2)}, u32[]{:S(2)}) collective-permute-start(bf16[256,1024]{1,0:T(8,128)(2,1)} %pad_maximum_fusion.1.tok_a), channel_id=1, source_target_pairs={{0,8},{1,9},{2,10},{3,11},{4,12},{5,13},{6,14},{7,15},{8,0},{9,1},... | collective-permute-start | bytes 1572872 | tf_op jit(solution)/shard_map/ppermute | solution.py:894
  107.6 120.0 %collective-permute-start.26 = (bf16[8,256,1024]{2,1,0:T(8,128)(2,1)}, bf16[8,256,1024]{2,1,0:T(8,128)(2,1)}, u32[]{:S(2)}, u32[]{:S(2)}) collective-permute-start(bf16[8,256,1024]{2,1,0:T(8,128)(2,1)} %copy-done.7), channel_id=1, source_target_pairs={{0,8},{1,9},{2,10},{3,11},{4,12},{5,13},{6,14},{7,15},{8,0},{9,1},... | collective-permute-start | bytes 12582920 | tf_op jit(solution)/shard_map/ppermute | solution.py:894
  107.6 91.9 %collective-permute-start.28 = (bf16[8,128,1024]{2,1,0:T(8,128)(2,1)}, bf16[8,128,1024]{2,1,0:T(8,128)(2,1)}, u32[]{:S(2)}, u32[]{:S(2)}) collective-permute-start(bf16[8,128,1024]{2,1,0:T(8,128)(2,1)} %collective-permute-done.27.refs_2_), channel_id=1, source_target_pairs={{0,1},{1,0},{2,3},{3,2},{4,5},{5,4},{6,7},{7,6},{8,9},{9,8},{10,11... | collective-permute-start | bytes 6291464 | tf_op jit(solution)/shard_map/ppermute | solution.py:894
  114.8 52.0 %collective-permute-start.20 = (bf16[3,128,1024]{2,1,0:T(8,128)(2,1)S(1)}, bf16[3,128,1024]{2,1,0:T(8,128)(2,1)S(1)}, u32[]{:S(2)}, u32[]{:S(2)}) collective-permute-start(bf16[3,128,1024]{2,1,0:T(8,128)(2,1)S(1)} %get-tuple-element.57), channel_id=1, source_target_pairs={{0,16},{1,17},{2,18},{3,19},{4,20},{5,21},{6,22},{7,23},{8,24},{9,... | collective-permute-start | bytes 2359304 | tf_op jit(solution)/shard_map/ppermute | solution.py:894
  117.8 41.3 %collective-permute-start.8 = (bf16[2,128,256]{2,1,0:T(8,128)(2,1)S(1)}, bf16[2,128,256]{2,1,0:T(8,128)(2,1)S(1)}, u32[]{:S(2)}, u32[]{:S(2)}) collective-permute-start(bf16[2,128,256]{2,1,0:T(8,128)(2,1)S(1)} %pad_maximum_fusion.9), channel_id=1, source_target_pairs={{0,1},{1,0},{2,3},{3,2},{4,5},{5,4},{6,7},{7,6},{8,9},{9,8},{10,11... | collective-permute-start | bytes 393224 | tf_op jit(solution)/shard_map/ppermute | solution.py:894
  122.0 59.5 %collective-permute-start.17 = (bf16[2,256,1024]{2,1,0:T(8,128)(2,1)S(1)}, bf16[2,256,1024]{2,1,0:T(8,128)(2,1)S(1)}, u32[]{:S(2)}, u32[]{:S(2)}) collective-permute-start(bf16[2,256,1024]{2,1,0:T(8,128)(2,1)S(1)} %mem_fwd.1), channel_id=1, source_target_pairs={{0,1},{1,0},{2,3},{3,2},{4,5},{5,4},{6,7},{7,6},{8,9},{9,8},{10,11... | collective-permute-start | bytes 3145736 | tf_op jit(solution)/shard_map/ppermute | solution.py:894
  166.8 31.3 %collective-permute-start.21 = (bf16[3,128,1024]{2,1,0:T(8,128)(2,1)S(1)}, bf16[3,128,1024]{2,1,0:T(8,128)(2,1)}, u32[]{:S(2)}, u32[]{:S(2)}) collective-permute-start(bf16[3,128,1024]{2,1,0:T(8,128)(2,1)S(1)} %collective-permute-done.20.refs_2_), channel_id=1, source_target_pairs={{0,1},{1,0},{2,3},{3,2},{4,5},{5,4},{6,7},{7,6},{8,9},{9,8},{10,11... | collective-permute-start | bytes 2359304 | tf_op jit(solution)/shard_map/ppermute | solution.py:894
  168.4 29.7 %collective-permute-start.22 = (bf16[3,128,1024]{2,1,0:T(8,128)(2,1)S(1)}, bf16[3,128,1024]{2,1,0:T(8,128)(2,1)S(1)}, u32[]{:S(2)}, u32[]{:S(2)}) collective-permute-start(bf16[3,128,1024]{2,1,0:T(8,128)(2,1)S(1)} %collective-permute-done.20.refs_2_), channel_id=1, source_target_pairs={{0,8},{1,9},{2,10},{3,11},{4,12},{5,13},{6,14},{7,15},{8,0},{9,1},... | collective-permute-start | bytes 2359304 | tf_op jit(solution)/shard_map/ppermute | solution.py:894
  199.0 28.6 %collective-permute-start.29 = (bf16[8,128,1024]{2,1,0:T(8,128)(2,1)}, bf16[8,128,1024]{2,1,0:T(8,128)(2,1)}, u32[]{:S(2)}, u32[]{:S(2)}) collective-permute-start(bf16[8,128,1024]{2,1,0:T(8,128)(2,1)} %collective-permute-done.27.refs_2_), channel_id=1, source_target_pairs={{0,8},{1,9},{2,10},{3,11},{4,12},{5,13},{6,14},{7,15},{8,0},{9,1},... | collective-permute-start | bytes 6291464 | tf_op jit(solution)/shard_map/ppermute | solution.py:894
  199.5 28.1 %collective-permute-start.30 = (bf16[8,128,1024]{2,1,0:T(8,128)(2,1)}, bf16[8,128,1024]{2,1,0:T(8,128)(2,1)}, u32[]{:S(2)}, u32[]{:S(2)}) collective-permute-start(bf16[8,128,1024]{2,1,0:T(8,128)(2,1)} %collective-permute-done.28.refs_3_), channel_id=1, source_target_pairs={{0,8},{1,9},{2,10},{3,11},{4,12},{5,13},{6,14},{7,15},{8,0},{9,1},... | collective-permute-start | bytes 6291464 | tf_op jit(solution)/shard_map/ppermute | solution.py:894
  262.5 66.6 %collective-permute-start.39 = (bf16[2,512,1024]{2,1,0:T(8,128)(2,1)}, bf16[2,512,1024]{2,1,0:T(8,128)(2,1)}, u32[]{:S(2)}, u32[]{:S(2)}) collective-permute-start(bf16[2,512,1024]{2,1,0:T(8,128)(2,1)} %get-tuple-element.78), channel_id=1, source_target_pairs={{0,8},{1,9},{2,10},{3,11},{4,12},{5,13},{6,14},{7,15},{8,0},{9,1},... | collective-permute-start | bytes 6291464 | tf_op jit(solution)/shard_map/ppermute | solution.py:894
  283.3 50.1 %collective-permute-start.35 = (bf16[256,1024]{1,0:T(8,128)(2,1)}, bf16[256,1024]{1,0:T(8,128)(2,1)}, u32[]{:S(2)}, u32[]{:S(2)}) collective-permute-start(bf16[256,1024]{1,0:T(8,128)(2,1)} %slice.177), channel_id=1, source_target_pairs={{0,8},{1,9},{2,10},{3,11},{4,12},{5,13},{6,14},{7,15},{8,0},{9,1},... | collective-permute-start | bytes 1572872 | tf_op jit(solution)/shard_map/ppermute | solution.py:894
  284.3 50.5 %collective-permute-start.31 = (bf16[64,1024]{1,0:T(8,128)(2,1)S(1)}, bf16[64,1024]{1,0:T(8,128)(2,1)S(1)}, u32[]{:S(2)}, u32[]{:S(2)}) collective-permute-start(bf16[64,1024]{1,0:T(8,128)(2,1)S(1)} %get-tuple-element.147), channel_id=1, source_target_pairs={{0,2},{1,3},{2,0},{3,1},{4,10},{5,11},{6,8},{7,9},{8,6},{9,7},{10,... | collective-permute-start | bytes 393224 | tf_op jit(solution)/shard_map/ppermute | solution.py:894
  284.6 50.2 %collective-permute-start.32 = (bf16[64,1024]{1,0:T(8,128)(2,1)S(1)}, bf16[64,1024]{1,0:T(8,128)(2,1)}, u32[]{:S(2)}, u32[]{:S(2)}) collective-permute-start(bf16[64,1024]{1,0:T(8,128)(2,1)S(1)} %get-tuple-element.148), channel_id=1, source_target_pairs={{0,0},{1,1},{2,2},{3,3},{4,8},{5,9},{6,10},{7,11},{8,4},{9,5},{10,... | collective-permute-start | bytes 393224 | tf_op jit(solution)/shard_map/ppermute | solution.py:894
  330.8 33.5 %collective-permute-start.40 = (bf16[2,256,1024]{2,1,0:T(8,128)(2,1)S(1)}, bf16[2,256,1024]{2,1,0:T(8,128)(2,1)S(1)}, u32[]{:S(2)}, u32[]{:S(2)}) collective-permute-start(bf16[2,256,1024]{2,1,0:T(8,128)(2,1)S(1)} %add_convert_fusion), channel_id=1, source_target_pairs={{0,1},{1,0},{2,3},{3,2},{4,5},{5,4},{6,7},{7,6},{8,9},{9,8},{10,11... | collective-permute-start | bytes 3145736 | tf_op jit(solution)/shard_map/ppermute | solution.py:894
  334.7 28.6 %collective-permute-start.36 = (bf16[128,1024]{1,0:T(8,128)(2,1)S(1)}, bf16[128,1024]{1,0:T(8,128)(2,1)S(1)}, u32[]{:S(2)}, u32[]{:S(2)}) collective-permute-start(bf16[128,1024]{1,0:T(8,128)(2,1)S(1)} %slice.252), channel_id=1, source_target_pairs={{0,1},{1,0},{2,3},{3,2},{4,5},{5,4},{6,7},{7,6},{8,9},{9,8},{10,11... | collective-permute-start | bytes 786440 | tf_op jit(solution)/shard_map/ppermute | solution.py:894
  368.5 66.8 %collective-permute-start.41 = (bf16[128,1024]{1,0:T(8,128)(2,1)S(1)}, bf16[128,1024]{1,0:T(8,128)(2,1)S(1)}, u32[]{:S(2)}, u32[]{:S(2)}) collective-permute-start(bf16[128,1024]{1,0:T(8,128)(2,1)S(1)} %get-tuple-element.133), channel_id=1, source_target_pairs={{0,2},{1,3},{2,0},{3,1},{4,10},{5,11},{6,8},{7,9},{8,6},{9,7},{10,... | collective-permute-start | bytes 786440 | tf_op jit(solution)/shard_map/ppermute | solution.py:894
  370.4 64.9 %collective-permute-start.42 = (bf16[128,1024]{1,0:T(8,128)(2,1)S(1)}, bf16[128,1024]{1,0:T(8,128)(2,1)S(1)}, u32[]{:S(2)}, u32[]{:S(2)}) collective-permute-start(bf16[128,1024]{1,0:T(8,128)(2,1)S(1)} %get-tuple-element.134), channel_id=1, source_target_pairs={{0,0},{1,1},{2,2},{3,3},{4,8},{5,9},{6,10},{7,11},{8,4},{9,5},{10,... | collective-permute-start | bytes 786440 | tf_op jit(solution)/shard_map/ppermute | solution.py:894
  (102 other events, 1461.7 us)
Sparse Core Ops, SparseCore 0:
  281.5 149.9 all-reduce.5
